TPU v7x, 32 devices: a whole 2x2x4 slice. The times are simulated.
32 devices in a mesh: groups: 2 (over y), space: 8 (over z, x), tm: 2 (over core).
Axes of the slice: x: 2, y: 2, z: 4, core: 2. Of those that a mesh axis runs over, the one named last changes fastest.
Arguments:
- incr: bfloat16 [16, 64, 8192], P(('groups', 'tm'), None, 'space'), parts along dimension 0, may hold values from -6 to 6
- costate: bfloat16 [16, 64, 8192], P(('groups', 'tm'), None, 'space'), parts along dimension 0, may hold values from -6 to 6
- lateral_mix: bfloat16 [9, 128, 128], replicated, may hold values from -0.5 to 0.5
- vertical_mix: bfloat16 [9, 64, 64], replicated, may hold values from -0.75 to 0.75
- neighbours: int32 [128, 9], P(('groups', 'space')), parts along dimension 0, may hold values from 0 to 63, as said below
- obs_lateral: bfloat16 [16, 128, 2048], P(('groups', 'tm'), None, 'space'), parts along dimension 0, may hold values from -0.5 to 0.5
- obs_vertical: bfloat16 [16, 64, 2048], P(('groups', 'tm'), None, 'space'), parts along dimension 0, may hold values from -0.75 to 0.75
- obs_weight: bfloat16 [16, 2048], P(('groups', 'tm'), 'space'), parts along dimension 0, may hold values from -24 to 24
- obs_block: int32 [16, 2048], P(('groups', 'tm'), 'space'), parts along dimension 0, may hold values from 0 to 7
- obs_count: int32 [16, 64], P(('groups', 'tm'), 'space'), parts along dimension 0, may hold values from 0 to 32, as said below
Outputs:
- model_residual: bfloat16 [16, 64, 8192], P(('groups', 'tm'), None, 'space'), parts along dimension 0
- adjoint_image: bfloat16 [16, 64, 8192], P(('groups', 'tm'), None, 'space'), parts along dimension 0
- obs_image: float32 [16, 2048], P(('groups', 'tm'), 'space'), parts along dimension 0
There are 2 independent parts, one for each index of `groups`. A program takes and returns all parts, laid end to end along the dimension named above; an argument that names none is the same for every part. Nothing has to cross between parts.
Inputs may be any that keep to these rules, and one draw needn't show every extreme that they name: `neighbours`: row b names blocks within 2 of b inside the grid; in one entry of each row the distance is exactly 2 unless the grid's end clips it. `obs_count`: in every subwindow one tile, drawn from the seed, has 32 live slots from every holder.
All inputs are finite; a program needn't handle non-finite values.
Results may differ from a plain program's by a relative error of at most 0.0047.
Values may be sent and summed in bfloat16 or wider, within the bound.
No kernel may reach another device: no remote copies, remote signals or barrier semaphores. Data moves between devices by JAX's collectives and lax.ppermute only.
A program may use at most 128 MiB of HBM per device.

v0:
```python
import functools

import jax
import jax.numpy as jnp
from jax import lax
from jax.experimental import pallas as pl
from jax.experimental.pallas import tpu as pltpu
from jax.sharding import PartitionSpec as P

REACH = 2
ROW_TILE = 16
BF16 = jnp.bfloat16
F32 = jnp.float32
VMEM = pl.BlockSpec(memory_space=pltpu.VMEM)
SMEM = pl.BlockSpec(memory_space=pltpu.SMEM)


def dot(a, b):
    return jnp.dot(a, b, preferred_element_type=F32)


def dot_nt(a, b):
    return lax.dot_general(a, b, (((1,), (1,)), ((), ())), preferred_element_type=F32)


def exchanged(array, pairs):
    both = [(a, b) for a, b in pairs] + [(b, a) for a, b in pairs]
    return lax.ppermute(array, "space", both)


def call(kernel, out_shape, args, specs, scratch=(), flops=0, moved=0, limit=None):
    multiple = isinstance(out_shape, (list, tuple))
    return pl.pallas_call(
        kernel,
        out_shape=out_shape,
        in_specs=specs,
        out_specs=[VMEM] * len(out_shape) if multiple else VMEM,
        scratch_shapes=list(scratch),
        compiler_params=pltpu.CompilerParams(vmem_limit_bytes=limit or 48 * 1024 * 1024),
        cost_estimate=pl.CostEstimate(flops=flops, bytes_accessed=moved, transcendentals=0),
    )(*args)


def pack_kernel(obs_lateral, obs_vertical, obs_weight, out):
    moments, cols, slots = obs_lateral.shape
    levels = obs_vertical.shape[1]
    tiles = out.shape[0]
    cap = slots // tiles
    tail = out.shape[1] - cols - levels
    for tile in range(tiles):
        lanes = slice(tile * cap, (tile + 1) * cap)
        out[tile, :cols] = jnp.concatenate([obs_lateral[s, :, lanes] for s in range(moments)], axis=1)
        out[tile, cols : cols + levels] = jnp.concatenate(
            [obs_vertical[s, :, lanes] for s in range(moments)], axis=1
        )
        row = jnp.concatenate([obs_weight[s : s + 1, lanes].astype(F32) for s in range(moments)], axis=1)
        out[tile, cols + levels :] = jnp.broadcast_to(row, (tail, row.shape[1])).astype(BF16)


def halo_kernel(info, incr, costate, crossed, neighbours, first, second):
    moments, levels, cols = incr.shape
    blocks = neighbours.shape[0]
    width = first.shape[1]
    odd = info[0]
    anchor = info[2]
    near = cols - width
    for target, lane in ((first, (1 - odd) * near), (second, odd * near)):
        lanes = pl.ds(pl.multiple_of(lane, 128), width)
        for k in range(moments - 1):
            target[k * levels : (k + 1) * levels] = incr[k, :, lanes]
            base = (moments - 1 + k) * levels
            target[base : base + levels] = costate[k + 1, :, lanes]
        base = 2 * (moments - 1) * levels
        target[base : base + levels] = crossed[:, lanes]
        base += levels
        own = lax.broadcasted_iota(jnp.int32, (blocks, neighbours.shape[1]), 0) + anchor
        offset = (neighbours[...] - own).astype(F32)
        target[base:] = jnp.zeros((target.shape[0] - base, width), BF16)
        tile = jnp.concatenate([offset, jnp.zeros((target.shape[0] - base - blocks, offset.shape[1]), F32)], axis=0)
        target[base:, : offset.shape[1]] = tile.astype(BF16)


def prepare_kernel(lateral_mix, vertical_mix, pair_fwd, pair_bwd, vert_fwd, vert_bwd):
    entries, cols, _ = lateral_mix.shape
    levels = vertical_mix.shape[1]
    pair_fwd[...] = jnp.zeros(pair_fwd.shape, BF16)
    pair_bwd[...] = jnp.zeros(pair_bwd.shape, BF16)
    for j in range(entries):
        at = slice((j % 2) * cols, (j % 2 + 1) * cols)
        pair_fwd[j // 2, at, at] = lateral_mix[j]
        pair_bwd[j // 2, at, at] = lateral_mix[j].astype(F32).T.astype(BF16)
    vert_fwd[...] = jnp.concatenate([vertical_mix[j] for j in range(entries)], axis=1)
    vert_bwd[...] = jnp.concatenate([vertical_mix[j].astype(F32).T.astype(BF16) for j in range(entries)], axis=1)


def mixed(get, count, blocks, entries, pair, vert, stage):
    levels = vert.shape[0]
    cols = pair.shape[1] // 2
    for k in range((entries + 1) // 2):
        single = 2 * k + 1 >= entries
        weight = pair[k, :cols, :cols] if single else pair[k]
        for s in range(count):
            rows = []
            for b in blocks:
                part = get(s, b, 2 * k)
                rows.append(part if single else jnp.concatenate([part, get(s, b, 2 * k + 1)], axis=1))
            result = dot(jnp.concatenate(rows, axis=0), weight).astype(BF16)
            for i in range(len(blocks)):
                piece = result[i * levels : (i + 1) * levels]
                lanes = slice(i * cols, (i + 1) * cols)
                stage[s, 2 * k * levels : (2 * k + 1) * levels, lanes] = piece[:, :cols]
                if not single:
                    stage[s, (2 * k + 1) * levels : (2 * k + 2) * levels, lanes] = piece[:, cols:]
    return [dot(vert[...], stage[s]) for s in range(count)]


def interior_kernel(
    info, near, incr, costate, crossed, pair_fwd, pair_bwd, vert_fwd, vert_bwd, residual, pulled, before, after, stage
):
    moments, levels, cols_all = incr.shape
    blocks, entries = near.shape
    cols = cols_all // blocks
    inner = list(range(REACH, blocks - REACH))
    lanes = slice(REACH * cols, (blocks - REACH) * cols)
    tm = info[1]
    anchor = info[2]
    gate = tm.astype(F32)
    before[...] = (crossed[...].astype(F32) * gate).astype(BF16)
    after[...] = (crossed[...].astype(F32) * (1.0 - gate)).astype(BF16)

    def forward(s, b, j):
        at = pl.ds(pl.multiple_of((near[b, j] - anchor) * cols, cols), cols)
        return before[:, at] if s == 0 else incr[s - 1, :, at]

    for s, pushed in enumerate(mixed(forward, moments, inner, entries, pair_fwd, vert_fwd, stage)):
        residual[s] = (incr[s, :, lanes].astype(F32) - pushed).astype(BF16)

    def backward(s, n, j):
        total = None
        for b in range(n - REACH, n + REACH + 1):
            at = slice(b * cols, (b + 1) * cols)
            source = after[:, at] if s == moments - 1 else costate[s + 1, :, at]
            term = jnp.where(near[b, j] == anchor + n, source, jnp.zeros_like(source))
            total = term if total is None else total + term
        return total

    for s, value in enumerate(mixed(backward, moments, inner, entries, pair_bwd, vert_bwd, stage)):
        pulled[s] = value


def final_kernel(
    packed, info, near, counts, incr, costate, crossed, first, second, arrived, owner,
    pair_fwd, pair_bwd, vert_fwd, vert_bwd, inner_residual, inner_pulled,
    residual, adjoint, image, before, after, stage, pulled, masked,
):
    moments, levels, cols_all = incr.shape
    blocks, entries = near.shape
    cols = cols_all // blocks
    width = REACH * cols
    odd = info[0]
    tm = info[1]
    anchor = info[2]
    gate = tm.astype(F32)
    outer = [b for b in range(blocks) if b < REACH or b >= blocks - REACH]
    inner_lanes = slice(width, cols_all - width)

    own = slice(width, width + cols_all)
    for s in range(moments):
        edge = 2 * (moments - 1) * levels if s == 0 else (s - 1) * levels
        if s == 0:
            before[s, :, own] = (crossed[...].astype(F32) * gate).astype(BF16)
        else:
            before[s, :, own] = incr[s - 1]
        rows = slice(edge, edge + levels)
        one, two = first[rows], second[rows]
        if s == 0:
            one, two = (one.astype(F32) * gate).astype(BF16), (two.astype(F32) * gate).astype(BF16)
        before[s, :, :width] = jnp.where(odd == 1, one, two)
        before[s, :, width + cols_all :] = jnp.where(odd == 1, two, one)
        last = s == moments - 1
        edge = (moments - 1 + (moments - 1 if last else s)) * levels
        rows = slice(edge, edge + levels)
        one, two = first[rows], second[rows]
        if last:
            one, two = (one.astype(F32) * (1.0 - gate)).astype(BF16), (two.astype(F32) * (1.0 - gate)).astype(BF16)
            after[s, :, own] = (crossed[...].astype(F32) * (1.0 - gate)).astype(BF16)
        else:
            after[s, :, own] = costate[s + 1]
        after[s, :, :width] = jnp.where(odd == 1, one, two)
        after[s, :, width + cols_all :] = jnp.where(odd == 1, two, one)

    def forward(s, b, j):
        at = pl.ds(pl.multiple_of((near[b, j] - anchor + REACH) * cols, cols), cols)
        return before[s, :, at]

    for s, pushed in enumerate(mixed(forward, moments, outer, entries, pair_fwd, vert_fwd, stage)):
        residual[s, :, :width] = (incr[s, :, :width].astype(F32) - pushed[:, :width]).astype(BF16)
        residual[s, :, inner_lanes] = inner_residual[s]
        residual[s, :, cols_all - width :] = (
            incr[s, :, cols_all - width :].astype(F32) - pushed[:, width:]
        ).astype(BF16)

    base = (2 * moments - 1) * levels
    one, two = first[base : base + ROW_TILE, :cols].astype(F32), second[base : base + ROW_TILE, :cols].astype(F32)
    left = jnp.where(odd == 1, one, two)
    right = jnp.where(odd == 1, two, one)

    def backward(s, n, j):
        total = None
        for b in range(n - REACH, n + REACH + 1):
            source = after[s, :, (b + REACH) * cols : (b + REACH + 1) * cols]
            if 0 <= b < blocks:
                term = jnp.where(near[b, j] == anchor + n, source, jnp.zeros_like(source))
            else:
                row = b + blocks if b < 0 else b - blocks
                offset = (left if b < 0 else right)[row : row + 1, j : j + 1]
                hit = jnp.where(offset == float(n - b), 1.0, 0.0)
                term = source * jnp.broadcast_to(hit, source.shape).astype(BF16)
            total = term if total is None else total + term
        return total

    for s, value in enumerate(mixed(backward, moments, outer, entries, pair_bwd, vert_bwd, stage)):
        pulled[s] = value

    tiles = counts.shape[1]
    slots = owner.shape[1]
    cap = slots // tiles
    slot = lax.broadcasted_iota(jnp.int32, (1, slots), 1)
    for s in range(moments):
        limit = jnp.zeros((1, slots), jnp.int32)
        for h in range(tiles):
            inside = (slot >= h * cap) & (slot < h * cap + counts[s, h])
            limit = jnp.where(inside, 1, limit)
        block = jnp.where(limit == 1, owner[s : s + 1], -1)
        if packed:
            part = slice(s * cap, (s + 1) * cap)
            whole = jnp.concatenate([arrived[h, :, part] for h in range(tiles)], axis=1)
        else:
            whole = arrived[s]
        lateral = whole[:cols]
        vertical = whole[cols : cols + levels].astype(F32)
        weight = whole[cols + levels : cols + levels + ROW_TILE].astype(F32)[:1]
        for b in range(blocks):
            hit = jnp.where(block == b, 1.0, 0.0)
            masked[b * cols : (b + 1) * cols] = lateral * jnp.broadcast_to(hit, lateral.shape).astype(BF16)
        along = dot(incr[s], masked[...])
        image[s : s + 1] = jnp.sum(vertical * along, axis=0, keepdims=True)
        scaled = (vertical * weight).astype(BF16)
        total = costate[s].astype(F32) + dot_nt(scaled, masked[...])
        adjoint[s, :, :width] = (total[:, :width] - pulled[s, :, :width]).astype(BF16)
        adjoint[s, :, inner_lanes] = (total[:, inner_lanes] - inner_pulled[s]).astype(BF16)
        adjoint[s, :, cols_all - width :] = (total[:, cols_all - width :] - pulled[s, :, width:]).astype(BF16)


def on_device(
    incr, costate, lateral_mix, vertical_mix, neighbours,
    obs_lateral, obs_vertical, obs_weight, obs_block, obs_count,
):
    moments, levels, cols_all = incr.shape
    entries, cols, _ = lateral_mix.shape
    blocks = neighbours.shape[0]
    slots = obs_block.shape[1]
    tiles = lax.axis_size("space")
    cap = slots // tiles
    width = REACH * cols
    place = lax.axis_index("space")
    tm = lax.axis_index("tm")
    info = jnp.stack([place % 2, tm, place * blocks]).astype(jnp.int32)
    shape = jax.ShapeDtypeStruct

    crossing = jnp.where(tm == 0, incr[-1], costate[0])
    crossed = lax.ppermute(crossing, "tm", [(0, 1), (1, 0)])

    height = cols + levels + ROW_TILE
    packed = moments * cap == 128
    if packed:
        outgoing = call(
            pack_kernel,
            shape((tiles, height, moments * cap), BF16),
            (obs_lateral, obs_vertical, obs_weight),
            [VMEM] * 3,
            moved=1 << 20,
        )
    else:
        stacked = jnp.concatenate(
            [obs_lateral, obs_vertical, jnp.broadcast_to(obs_weight[:, None], (moments, ROW_TILE, slots))], axis=1
        )
        outgoing = stacked.reshape(moments, height, tiles, cap).transpose(2, 1, 0, 3).reshape(tiles, height, -1)

    halo = shape(((2 * moments - 1) * levels + ROW_TILE, width), BF16)
    first, second = call(
        halo_kernel, [halo, halo], (info, incr, costate, crossed, neighbours), [SMEM] + [VMEM] * 4, moved=1 << 20
    )
    first = exchanged(first, [(i, i + 1) for i in range(0, tiles - 1, 2)])
    second = exchanged(second, [(i, i + 1) for i in range(1, tiles - 1, 2)])

    arrived = lax.all_to_all(outgoing, "space", split_axis=0, concat_axis=0, tiled=True)
    if not packed:
        arrived = arrived.reshape(tiles, height, moments, cap).transpose(2, 1, 0, 3).reshape(moments, height, slots)

    pairs = (entries + 1) // 2
    weights = call(
        prepare_kernel,
        [shape((pairs, 2 * cols, 2 * cols), BF16)] * 2 + [shape((levels, entries * levels), BF16)] * 2,
        (lateral_mix, vertical_mix),
        [VMEM] * 2,
        moved=1 << 21,
    )

    inner = (blocks - 2 * REACH) * cols
    stage = pltpu.VMEM((moments, entries * levels, inner), BF16)
    inner_residual, inner_pulled = call(
        interior_kernel,
        [shape((moments, levels, inner), BF16), shape((moments, levels, inner), F32)],
        (info, neighbours, incr, costate, crossed, *weights),
        [SMEM] * 2 + [VMEM] * 7,
        scratch=[pltpu.VMEM((levels, cols_all), BF16)] * 2 + [stage],
        flops=2_000_000_000,
        moved=4 << 20,
    )

    outer = pltpu.VMEM((moments, entries * levels, 2 * width), BF16)
    residual, adjoint, image = call(
        functools.partial(final_kernel, packed),
        [shape(incr.shape, BF16), shape(incr.shape, BF16), shape((moments, slots), F32)],
        (
            info, neighbours, obs_count, incr, costate, crossed, first, second, arrived, obs_block,
            *weights, inner_residual, inner_pulled,
        ),
        [SMEM] * 3 + [VMEM] * 13,
        scratch=[pltpu.VMEM((moments, levels, cols_all + 2 * width), BF16)] * 2
        + [outer, pltpu.VMEM((moments, levels, 2 * width), F32), pltpu.VMEM((cols_all, slots), BF16)],
        flops=2_000_000_000,
        moved=6 << 20,
    )
    return residual, adjoint, image


def solution(mesh):
    fields = P(("groups", "tm"), None, "space")
    rows = P(("groups", "tm"), "space")
    in_specs = (
        fields, fields, P(), P(), P(("groups", "space"), None), fields, fields, rows, rows, rows,
    )
    return jax.shard_map(
        on_device, mesh=mesh, in_specs=in_specs, out_specs=(fields, fields, rows), check_vma=False
    )
```

profile of v0, /device:TPU:9, one launch (start us, length us, event | category | flops | bytes accessed | tf_op | source)
XLA Modules:
  0.0 37.5 jit_solution(12678821693429106105)
XLA Ops:
  0.6 0.0 copy-start.3
  0.6 0.9 %copy-done.3 = bf16[4,128,256]{2,1,0:T(8,128)(2,1)S(1)} copy-done((bf16[4,128,256]{2,1,0:T(8,128)(2,1)S(1)}, bf16[4,128,256]{2,1,0:T(8,128)(2,1)}, u32[]{:S(2)}) %copy-start.3) | copy-done | bytes 262168
  1.6 0.0 copy-start.5
  1.6 0.9 %copy-done.5 = bf16[4,64,256]{2,1,0:T(8,128)(2,1)S(1)} copy-done((bf16[4,64,256]{2,1,0:T(8,128)(2,1)S(1)}, bf16[4,64,256]{2,1,0:T(8,128)(2,1)}, u32[]{:S(2)}) %copy-start.5) | copy-done | bytes 131096
  2.5 0.0 copy-start.7
  2.5 0.7 %copy-done.7 = bf16[4,256]{1,0:T(4,128)(2,1)S(1)} copy-done((bf16[4,256]{1,0:T(4,128)(2,1)S(1)}, bf16[4,256]{1,0:T(4,128)(2,1)}, u32[]{:S(2)}) %copy-start.7) | copy-done | bytes 2072
  3.2 0.0 copy-start.1
  3.2 1.2 %shard_map.122 = bf16[8,208,128]{2,1,0:T(8,128)(2,1)} custom-call(bf16[4,128,256]{2,1,0:T(8,128)(2,1)S(1)} %copy-done.3, bf16[4,64,256]{2,1,0:T(8,128)(2,1)S(1)} %copy-done.5, bf16[4,256]{1,0:T(4,128)(2,1)S(1)} %copy-done.7), custom_call_target="tpu_custom_call" | custom-call | bytes 1048576 | tf_op jit(solution)/shard_map/pallas_call | solution.py:33
  4.3 0.0 copy-start
  4.3 5.8 %all-to-all-start = ((bf16[8,208,128]{2,1,0:T(8,128)(2,1)}), bf16[8,208,128]{2,1,0:T(8,128)(2,1)S(1)}, u32[]{:S(2)}, u32[]{:S(2)}) async-start(bf16[8,208,128]{2,1,0:T(8,128)(2,1)} %shard_map.122), calls=%async_computation | async-start | bytes 851968 | tf_op jit(solution)/shard_map/all_to_all | solution.py:297
  10.2 0.0 copy-done.1
  10.2 0.0 copy-done
  10.2 1.3 %collective-permute-start = (bf16[64,1024]{1,0:T(8,128)(2,1)S(1)}, bf16[64,1024]{1,0:T(8,128)(2,1)S(1)}, u32[]{:S(2)}, u32[]{:S(2)}) collective-permute-start(bf16[64,1024]{1,0:T(8,128)(2,1)S(1)} %select_bitcast_fusion), channel_id=1, source_target_pairs={{0,1},{1,0},{2,3},{3,2},{4,5},{5,4},{6,7},{7,6},{8,9},{9,8},{10,11... | collective-permute-start | bytes 393224 | tf_op jit(solution)/shard_map/ppermute | solution.py:272
  11.5 0.0 copy-start.6
  11.5 0.1 pad_add_fusion.info
  11.6 0.0 copy-start.2
  11.6 0.0 copy-start.4
  11.6 0.9 %collective-permute-done.crossed = bf16[64,1024]{1,0:T(8,128)(2,1)S(1)} collective-permute-done((bf16[64,1024]{1,0:T(8,128)(2,1)S(1)}, bf16[64,1024]{1,0:T(8,128)(2,1)S(1)}, u32[]{:S(2)}, u32[]{:S(2)}) %collective-permute-start) | collective-permute-done | bytes 131104 | tf_op jit(solution)/shard_map/ppermute | solution.py:272
  12.5 0.0 copy-done.6
  12.5 0.6 %shard_map.121 = (bf16[464,256]{1,0:T(8,128)(2,1)S(1)}, bf16[464,256]{1,0:T(8,128)(2,1)S(1)}) custom-call(s32[3]{0:T(128)S(1)} %pad_add_fusion.info, bf16[4,64,1024]{2,1,0:T(8,128)(2,1)S(1)} %copy-done, bf16[4,64,1024]{2,1,0:T(8,128)(2,1)S(1)} %copy-done.1, bf16[64,1024]{1,0:T(8,128)(2,1)S(1)} %collective-permute-done.crossed, s32[8,9]{1,0:T(8,128)S(1)} %copy-done.6), custom_call_target="tpu_custom_call" | custom-call | bytes 1048576 | tf_op jit(solution)/shard_map/pallas_call | solution.py:33
  13.1 1.2 %collective-permute-start.1 = (bf16[464,256]{1,0:T(8,128)(2,1)S(1)}, bf16[464,256]{1,0:T(8,128)(2,1)S(1)}, u32[]{:S(2)}, u32[]{:S(2)}) collective-permute-start(bf16[464,256]{1,0:T(8,128)(2,1)S(1)} %get-tuple-element.11), channel_id=1, source_target_pairs={{0,2},{4,6},{8,10},{12,14},{2,0},{6,4},{10,8},{14,12},{1,3},{5,7},... | collective-permute-start | bytes 712712 | tf_op jit(solution)/shard_map/ppermute | solution.py:28
  14.3 1.9 %collective-permute-start.2 = (bf16[464,256]{1,0:T(8,128)(2,1)S(1)}, bf16[464,256]{1,0:T(8,128)(2,1)S(1)}, u32[]{:S(2)}, u32[]{:S(2)}) collective-permute-start(bf16[464,256]{1,0:T(8,128)(2,1)S(1)} %get-tuple-element.12), channel_id=1, source_target_pairs={{2,4},{6,8},{10,12},{4,2},{8,6},{12,10},{3,5},{7,9},{11,13},{5,3},... | collective-permute-start | bytes 712712 | tf_op jit(solution)/shard_map/ppermute | solution.py:28
  16.3 0.0 copy-done.2
  16.3 0.0 copy-done.4
  16.3 0.3 shard_map.123
  16.6 0.0 copy-start.8
  16.6 0.0 copy-start.10
  16.6 4.3 %shard_map.124 = (bf16[4,64,512]{2,1,0:T(8,128)(2,1)S(1)}, f32[4,64,512]{2,1,0:T(8,128)S(1)}) custom-call(s32[3]{0:T(128)S(1)} %pad_add_fusion.info, s32[8,9]{1,0:T(8,128)S(1)} %copy-done.6, bf16[4,64,1024]{2,1,0:T(8,128)(2,1)S(1)} %copy-done, bf16[4,64,1024]{2,1,0:T(8,128)(2,1)S(1)} %copy-done.1, bf16[64,1024]{1,0:T(8,128)(2,1)S(1)} %collective-permute-done.crossed, ...), custom_call_target="tpu_custom_call" | custom-call | flops 2000000000 | bytes 4194304 | tf_op jit(solution)/shard_map/pallas_call | solution.py:33
  20.9 0.0 copy-done.8
  21.0 0.0 copy-start.12
  21.0 0.8 %copy-done.12 = f32[4,64,512]{2,1,0:T(8,128)} copy-done((f32[4,64,512]{2,1,0:T(8,128)}, f32[4,64,512]{2,1,0:T(8,128)S(1)}, u32[]{:S(2)}) %copy-start.12) | copy-done | bytes 524312
  21.8 0.0 copy-start.14
  21.8 0.7 %copy-done.14 = bf16[4,64,512]{2,1,0:T(8,128)(2,1)} copy-done((bf16[4,64,512]{2,1,0:T(8,128)(2,1)}, bf16[4,64,512]{2,1,0:T(8,128)(2,1)S(1)}, u32[]{:S(2)}) %copy-start.14) | copy-done | bytes 262168
  22.5 0.0 copy-start.11
  22.5 6.1 %collective-permute-done.1.first = bf16[464,256]{1,0:T(8,128)(2,1)S(1)} collective-permute-done((bf16[464,256]{1,0:T(8,128)(2,1)S(1)}, bf16[464,256]{1,0:T(8,128)(2,1)S(1)}, u32[]{:S(2)}, u32[]{:S(2)}) %collective-permute-start.1) | collective-permute-done | bytes 237600 | tf_op jit(solution)/shard_map/ppermute | solution.py:28
  28.5 0.0 collective-permute-done.2.second
  28.5 0.0 all-to-all-done.arrived
  28.5 0.0 copy-done.10
  28.5 0.0 copy-done.11
  28.5 0.0 copy-start.9
  28.5 0.9 %copy-done.9 = bf16[64,576]{1,0:T(8,128)(2,1)S(1)} copy-done((bf16[64,576]{1,0:T(8,128)(2,1)S(1)}, bf16[64,576]{1,0:T(8,128)(2,1)}, u32[]{:S(2)}) %copy-start.9) | copy-done | bytes 73752
  29.4 0.0 copy-start.13
  29.4 1.0 %copy-done.13 = f32[4,64,512]{2,1,0:T(8,128)S(1)} copy-done((f32[4,64,512]{2,1,0:T(8,128)S(1)}, f32[4,64,512]{2,1,0:T(8,128)}, u32[]{:S(2)}) %copy-start.13) | copy-done | bytes 524312
  30.5 0.0 copy-start.15
  30.5 0.9 %copy-done.15 = bf16[4,64,512]{2,1,0:T(8,128)(2,1)S(1)} copy-done((bf16[4,64,512]{2,1,0:T(8,128)(2,1)S(1)}, bf16[4,64,512]{2,1,0:T(8,128)(2,1)}, u32[]{:S(2)}) %copy-start.15) | copy-done | bytes 262168
  31.4 6.0 %shard_map.125 = (bf16[4,64,1024]{2,1,0:T(8,128)(2,1)}, bf16[4,64,1024]{2,1,0:T(8,128)(2,1)}, f32[4,256]{1,0:T(4,128)}) custom-call(s32[3]{0:T(128)S(1)} %pad_add_fusion.info, s32[8,9]{1,0:T(8,128)S(1)} %copy-done.6, s32[4,8]{1,0:T(4,128)S(1)} %copy-done.11, bf16[4,64,1024]{2,1,0:T(8,128)(2,1)S(1)} %copy-done, bf16[4,64,1024]{2,1,0:T(8,128)(2,1)S(1)} %copy-done.1, ...), custom_call_target="tpu_custom_call" | custom-call | flops 2000000000 | bytes 6291456 | tf_op jit(solution)/shard_map/pallas_call | solution.py:33
  (1 shorter events, 0.0 us)
Async XLA Ops:
  0.6 1.0 %copy-start.3 = (bf16[4,128,256]{2,1,0:T(8,128)(2,1)S(1)}, bf16[4,128,256]{2,1,0:T(8,128)(2,1)}, u32[]{:S(2)}) copy-start(bf16[4,128,256]{2,1,0:T(8,128)(2,1)} %obs_lateral.1) | copy-start | bytes 786436
  1.6 0.9 %copy-start.5 = (bf16[4,64,256]{2,1,0:T(8,128)(2,1)S(1)}, bf16[4,64,256]{2,1,0:T(8,128)(2,1)}, u32[]{:S(2)}) copy-start(bf16[4,64,256]{2,1,0:T(8,128)(2,1)} %obs_vertical.1) | copy-start | bytes 393220
  2.5 0.7 %copy-start.7 = (bf16[4,256]{1,0:T(4,128)(2,1)S(1)}, bf16[4,256]{1,0:T(4,128)(2,1)}, u32[]{:S(2)}) copy-start(bf16[4,256]{1,0:T(4,128)(2,1)} %obs_weight.1) | copy-start | bytes 6148
  3.2 7.0 %copy-start.1 = (bf16[4,64,1024]{2,1,0:T(8,128)(2,1)S(1)}, bf16[4,64,1024]{2,1,0:T(8,128)(2,1)}, u32[]{:S(2)}) copy-start(bf16[4,64,1024]{2,1,0:T(8,128)(2,1)} %costate.5) | copy-start | bytes 1572868
  4.3 5.8 %copy-start = (bf16[4,64,1024]{2,1,0:T(8,128)(2,1)S(1)}, bf16[4,64,1024]{2,1,0:T(8,128)(2,1)}, u32[]{:S(2)}) copy-start(bf16[4,64,1024]{2,1,0:T(8,128)(2,1)} %incr.5) | copy-start | bytes 1572868
  4.3 24.2 %all-to-all-start = ((bf16[8,208,128]{2,1,0:T(8,128)(2,1)}), bf16[8,208,128]{2,1,0:T(8,128)(2,1)S(1)}, u32[]{:S(2)}, u32[]{:S(2)}) async-start(bf16[8,208,128]{2,1,0:T(8,128)(2,1)} %shard_map.122), calls=%async_computation | async-start | bytes 851968 | tf_op jit(solution)/shard_map/all_to_all | solution.py:297
  10.2 2.3 %collective-permute-start = (bf16[64,1024]{1,0:T(8,128)(2,1)S(1)}, bf16[64,1024]{1,0:T(8,128)(2,1)S(1)}, u32[]{:S(2)}, u32[]{:S(2)}) collective-permute-start(bf16[64,1024]{1,0:T(8,128)(2,1)S(1)} %select_bitcast_fusion), channel_id=1, source_target_pairs={{0,1},{1,0},{2,3},{3,2},{4,5},{5,4},{6,7},{7,6},{8,9},{9,8},{10,11... | collective-permute-start | bytes 393224 | tf_op jit(solution)/shard_map/ppermute | solution.py:272
  11.5 1.0 %copy-start.6 = (s32[8,9]{1,0:T(8,128)S(1)}, s32[8,9]{1,0:T(8,128)}, u32[]{:S(2)}) copy-start(s32[8,9]{1,0:T(8,128)} %near.3) | copy-start | bytes 868
  11.6 4.7 %copy-start.2 = (bf16[9,128,128]{2,1,0:T(8,128)(2,1)S(1)}, bf16[9,128,128]{2,1,0:T(8,128)(2,1)}, u32[]{:S(2)}) copy-start(bf16[9,128,128]{2,1,0:T(8,128)(2,1)} %lateral_mix.1) | copy-start | bytes 884740
  11.6 4.7 %copy-start.4 = (bf16[9,64,64]{2,1,0:T(8,128)(2,1)S(1)}, bf16[9,64,64]{2,1,0:T(8,128)(2,1)}, u32[]{:S(2)}) copy-start(bf16[9,64,64]{2,1,0:T(8,128)(2,1)} %vertical_mix.1) | copy-start | bytes 221188
  13.1 15.4 %collective-permute-start.1 = (bf16[464,256]{1,0:T(8,128)(2,1)S(1)}, bf16[464,256]{1,0:T(8,128)(2,1)S(1)}, u32[]{:S(2)}, u32[]{:S(2)}) collective-permute-start(bf16[464,256]{1,0:T(8,128)(2,1)S(1)} %get-tuple-element.11), channel_id=1, source_target_pairs={{0,2},{4,6},{8,10},{12,14},{2,0},{6,4},{10,8},{14,12},{1,3},{5,7},... | collective-permute-start | bytes 712712 | tf_op jit(solution)/shard_map/ppermute | solution.py:28
  14.3 14.2 %collective-permute-start.2 = (bf16[464,256]{1,0:T(8,128)(2,1)S(1)}, bf16[464,256]{1,0:T(8,128)(2,1)S(1)}, u32[]{:S(2)}, u32[]{:S(2)}) collective-permute-start(bf16[464,256]{1,0:T(8,128)(2,1)S(1)} %get-tuple-element.12), channel_id=1, source_target_pairs={{2,4},{6,8},{10,12},{4,2},{8,6},{12,10},{3,5},{7,9},{11,13},{5,3},... | collective-permute-start | bytes 712712 | tf_op jit(solution)/shard_map/ppermute | solution.py:28
  16.6 4.3 %copy-start.8 = (bf16[64,576]{1,0:T(8,128)(2,1)}, bf16[64,576]{1,0:T(8,128)(2,1)S(1)}, u32[]{:S(2)}) copy-start(bf16[64,576]{1,0:T(8,128)(2,1)S(1)} %get-tuple-element.16.vert_bwd) | copy-start | bytes 221188
  16.6 11.9 %copy-start.10 = (s32[4,256]{1,0:T(4,128)S(1)}, s32[4,256]{1,0:T(4,128)}, u32[]{:S(2)}) copy-start(s32[4,256]{1,0:T(4,128)} %owner.1) | copy-start | bytes 12292
  21.0 0.8 %copy-start.12 = (f32[4,64,512]{2,1,0:T(8,128)}, f32[4,64,512]{2,1,0:T(8,128)S(1)}, u32[]{:S(2)}) copy-start(f32[4,64,512]{2,1,0:T(8,128)S(1)} %get-tuple-element.18.inner_pulled) | copy-start | bytes 1572868
  21.8 0.7 %copy-start.14 = (bf16[4,64,512]{2,1,0:T(8,128)(2,1)}, bf16[4,64,512]{2,1,0:T(8,128)(2,1)S(1)}, u32[]{:S(2)}) copy-start(bf16[4,64,512]{2,1,0:T(8,128)(2,1)S(1)} %get-tuple-element.17.inner_residual) | copy-start | bytes 786436
  22.5 6.1 %copy-start.11 = (s32[4,8]{1,0:T(4,128)S(1)}, s32[4,8]{1,0:T(4,128)}, u32[]{:S(2)}) copy-start(s32[4,8]{1,0:T(4,128)} %counts.1) | copy-start | bytes 388
  28.5 0.9 %copy-start.9 = (bf16[64,576]{1,0:T(8,128)(2,1)S(1)}, bf16[64,576]{1,0:T(8,128)(2,1)}, u32[]{:S(2)}) copy-start(bf16[64,576]{1,0:T(8,128)(2,1)} %copy-done.8) | copy-start | bytes 221188
  29.4 1.0 %copy-start.13 = (f32[4,64,512]{2,1,0:T(8,128)S(1)}, f32[4,64,512]{2,1,0:T(8,128)}, u32[]{:S(2)}) copy-start(f32[4,64,512]{2,1,0:T(8,128)} %copy-done.12) | copy-start | bytes 1572868
  30.5 0.9 %copy-start.15 = (bf16[4,64,512]{2,1,0:T(8,128)(2,1)S(1)}, bf16[4,64,512]{2,1,0:T(8,128)(2,1)}, u32[]{:S(2)}) copy-start(bf16[4,64,512]{2,1,0:T(8,128)(2,1)} %copy-done.14) | copy-start | bytes 786436
where the time goes:
time: 37.9 us; the launch traced here: 37.5 us
  Pallas kernels  12.4 us (33%)
  starting transfers between devices  10.3 us (27%)
  waiting for transfers between devices  6.97 us (18%)
  local copies, waits for them, and re-layouts  6.92 us (18%)
  between operations  0.76 us (2%)
    pallas_call x5, Pallas kernels, call(): pl.pallas_call(kernel, out_shape=out_shape, in_specs=specs, out_specs=[VM...  12.4 us
    unnamed x32, local copies, waits for them, and re-layouts  6.92 us
    ppermute x2, waiting for transfers between devices, exchanged(): return lax.ppermute(array, 'space', both)  6.06 us
    all_to_all x1, starting transfers between devices, on_device(): lax.all_to_all(outgoing, 'space', split_axis=0, concat_axis=0, tiled=True)  5.82 us
    ppermute x2, starting transfers between devices, exchanged(): return lax.ppermute(array, 'space', both)  3.17 us
    ppermute x1, starting transfers between devices, on_device(): crossed = lax.ppermute(crossing, 'tm', [(0, 1), (1, 0)])  1.3 us
    ppermute x1, waiting for transfers between devices, on_device(): crossed = lax.ppermute(crossing, 'tm', [(0, 1), (1, 0)])  0.9 us
  transfers between devices with their start and end apart: 4, of which 2 were waited for; matrix products, arithmetic and copies ran while one was open for 0% of the time, Pallas kernels for 14%

commit v1 on v0

v1 whole, which is shorter than its diff:
```python
import functools

import jax
import jax.numpy as jnp
from jax import lax
from jax.experimental import pallas as pl
from jax.experimental.pallas import tpu as pltpu
from jax.sharding import PartitionSpec as P

REACH = 2
ROW_TILE = 16
FULL = 63.6
BF16 = jnp.bfloat16
F32 = jnp.float32
VMEM = pl.BlockSpec(memory_space=pltpu.VMEM)
ANY = pl.BlockSpec(memory_space=pl.ANY)
HBM = pl.BlockSpec(memory_space=pltpu.HBM)
SMEM = pl.BlockSpec(memory_space=pltpu.SMEM)


def dot(a, b):
    return jnp.dot(a, b, preferred_element_type=F32)


def dot_nt(a, b):
    return lax.dot_general(a, b, (((1,), (1,)), ((), ())), preferred_element_type=F32)


def exchanged(array, pairs):
    both = [(a, b) for a, b in pairs] + [(b, a) for a, b in pairs]
    return lax.ppermute(array, "space", both)


def call(kernel, out_shape, args, specs, out_specs=None, scratch=(), cost=0, limit=16, aliases=None):
    multiple = isinstance(out_shape, (list, tuple))
    return pl.pallas_call(
        kernel,
        out_shape=out_shape,
        in_specs=specs,
        out_specs=out_specs or ([VMEM] * len(out_shape) if multiple else VMEM),
        scratch_shapes=list(scratch),
        input_output_aliases=aliases or {},
        compiler_params=pltpu.CompilerParams(vmem_limit_bytes=int(limit * 1024 * 1024)),
        cost_estimate=pl.CostEstimate(flops=cost * 1_000_000_000, bytes_accessed=cost * 1_000_000, transcendentals=0),
    )(*args)


def gated(data, after):
    return call(gate_kernel, jax.ShapeDtypeStruct(data.shape, BF16), (data, after), [ANY] * 2, ANY, limit=1, aliases={0: 0})


def fetched(pairs, sems):
    copies = [pltpu.make_async_copy(source, target, sems.at[k]) for k, (source, target) in enumerate(pairs)]
    for copy in copies:
        copy.start()
    return copies


def edges_kernel(near_any, incr, costate, crossed, first, second, near, near_sem, sems):
    moments, levels, cols = incr.shape
    blocks, entries = near.shape
    width = first.shape[1]
    place = lax.axis_index("space")
    odd = lax.rem(place, 2)
    fetch = pltpu.make_async_copy(near_any, near, near_sem)
    fetch.start()
    slabs = [incr.at[k] for k in range(moments - 1)] + [costate.at[k] for k in range(1, moments)] + [crossed]
    pairs = []
    for target, right in ((first, 1 - odd), (second, odd)):
        lanes = pl.ds(pl.multiple_of(right * (cols - width), 128), width)
        pairs += [(slab.at[:, lanes], target.at[pl.ds(k * levels, levels)]) for k, slab in enumerate(slabs)]
    copies = fetched(pairs, sems)
    fetch.wait()
    own = lax.broadcasted_iota(jnp.int32, near.shape, 0) + place * blocks
    distance = (near[...] - own).astype(F32)
    distance = jnp.concatenate([distance, jnp.zeros((ROW_TILE - blocks, entries), F32)], axis=0).astype(BF16)
    for target in (first, second):
        target[len(slabs) * levels :] = jnp.zeros((ROW_TILE, width), BF16)
        target[len(slabs) * levels :, :entries] = distance
    for copy in copies:
        copy.wait()


def pack_kernel(lateral_any, vertical_any, weight_any, out, obs_lateral, obs_vertical, obs_weight, sems):
    copies = fetched(
        [(lateral_any, obs_lateral), (vertical_any, obs_vertical), (weight_any, obs_weight)], sems
    )
    for copy in copies:
        copy.wait()
    moments, cols, slots = obs_lateral.shape
    levels = obs_vertical.shape[1]
    tiles = out.shape[0]
    cap = slots // tiles
    for tile in range(tiles):
        lanes = slice(tile * cap, (tile + 1) * cap)
        out[tile, :cols] = jnp.concatenate([obs_lateral[s, :, lanes] for s in range(moments)], axis=1)
        out[tile, cols : cols + levels] = jnp.concatenate(
            [obs_vertical[s, :, lanes] for s in range(moments)], axis=1
        )
        row = jnp.concatenate([obs_weight[s : s + 1, lanes].astype(F32) for s in range(moments)], axis=1)
        out[tile, cols + levels :] = jnp.broadcast_to(row, (ROW_TILE, row.shape[1])).astype(BF16)


def gate_kernel(data, after, out):
    pass


def mixed(get, moments, blocks, entries, pair, vert, stage):
    levels = vert.shape[0]
    cols = pair.shape[1] // 2
    for k in range((entries + 1) // 2):
        single = 2 * k + 1 >= entries
        weight = pair[k, :cols, :cols] if single else pair[k]
        for s in moments:
            rows = []
            for b in blocks:
                part = get(s, b, 2 * k)
                rows.append(part if single else jnp.concatenate([part, get(s, b, 2 * k + 1)], axis=1))
            result = dot(jnp.concatenate(rows, axis=0), weight).astype(BF16)
            for i in range(len(blocks)):
                piece = result[i * levels : (i + 1) * levels]
                lanes = slice(i * cols, (i + 1) * cols)
                stage[s, 2 * k * levels : (2 * k + 1) * levels, lanes] = piece[:, :cols]
                if not single:
                    stage[s, (2 * k + 1) * levels : (2 * k + 2) * levels, lanes] = piece[:, cols:]
    return [(s, dot(vert[...], stage[s])) for s in moments]


def interior_kernel(
    near, counts, incr, costate, crossed, lateral_mix, vertical_mix, owner,
    residual, base, pair_fwd, pair_bwd, vert_fwd, vert_bwd, target, stage,
):
    moments, levels, cols_all = incr.shape
    blocks, entries = near.shape
    cols = cols_all // blocks
    inner = list(range(REACH, blocks - REACH))
    lanes = slice(REACH * cols, (blocks - REACH) * cols)
    tm = lax.axis_index("tm")
    anchor = lax.axis_index("space") * blocks

    pair_fwd[...] = jnp.zeros(pair_fwd.shape, BF16)
    pair_bwd[...] = jnp.zeros(pair_bwd.shape, BF16)
    for j in range(entries):
        at = slice((j % 2) * cols, (j % 2 + 1) * cols)
        pair_fwd[j // 2, at, at] = lateral_mix[j]
        pair_bwd[j // 2, at, at] = lateral_mix[j].astype(F32).T.astype(BF16)
    vert_fwd[...] = jnp.concatenate([vertical_mix[j] for j in range(entries)], axis=1)
    vert_bwd[...] = jnp.concatenate([vertical_mix[j].astype(F32).T.astype(BF16) for j in range(entries)], axis=1)

    tiles = counts.shape[1]
    cap = owner.shape[1] // tiles
    slot = lax.broadcasted_iota(jnp.int32, (1, owner.shape[1]), 1)
    for s in range(moments):
        live = jnp.zeros(slot.shape, jnp.int32)
        for h in range(tiles):
            inside = (slot >= h * cap) & (slot < h * cap + counts[s, h])
            live = jnp.where(inside, 1, live)
        target[s : s + 1] = jnp.where(live == 1, owner[s : s + 1], -1)

    def forward(s, b, j):
        at = pl.ds(pl.multiple_of((near[b, j] - anchor) * cols, cols), cols)
        return crossed[:, at] if s == 0 else incr[s - 1, :, at]

    def backward(s, n, j):
        total = None
        for b in range(n - REACH, n + REACH + 1):
            at = slice(b * cols, (b + 1) * cols)
            source = crossed[:, at] if s == moments - 1 else costate[s + 1, :, at]
            term = jnp.where(near[b, j] == anchor + n, source, jnp.zeros_like(source))
            total = term if total is None else total + term
        return total

    def run_forward(which):
        for s, pushed in mixed(forward, which, inner, entries, pair_fwd, vert_fwd, stage):
            residual[s] = (incr[s, :, lanes].astype(F32) - pushed).astype(BF16)

    def run_backward(which):
        for s, value in mixed(backward, which, inner, entries, pair_bwd, vert_bwd, stage):
            base[s] = costate[s, :, lanes].astype(F32) - value

    @pl.when(tm == 0)
    def _():
        residual[0] = incr[0, :, lanes]
        run_backward([moments - 1])

    @pl.when(tm == 1)
    def _():
        run_forward([0])
        base[moments - 1] = costate[moments - 1, :, lanes].astype(F32)

    run_forward(range(1, moments))
    run_backward(range(moments - 1))


def edge_kernel(
    near, incr, costate, crossed, first, second, pair_fwd, pair_bwd, vert_fwd, vert_bwd, inner_residual,
    residual_any, base, residual, before, after, stage, sems,
):
    moments, levels, cols_all = incr.shape
    blocks, entries = near.shape
    cols = cols_all // blocks
    width = REACH * cols
    place = lax.axis_index("space")
    odd = lax.rem(place, 2)
    tm = lax.axis_index("tm")
    anchor = place * blocks
    outer = [b for b in range(blocks) if b < REACH or b >= blocks - REACH]
    reach_cols = 3 * width

    def fill(target, s, source, edge):
        rows = slice(edge * levels, (edge + 1) * levels)
        one, two = first[rows], second[rows]
        target[s, :, :width] = jnp.where(odd == 1, one, two)
        target[s, :, width:reach_cols] = source[:, : 2 * width]
        target[s, :, reach_cols : reach_cols + 2 * width] = source[:, cols_all - 2 * width :]
        target[s, :, reach_cols + 2 * width :] = jnp.where(odd == 1, two, one)

    for s in range(moments - 1):
        fill(before, s + 1, incr[s], s)
        fill(after, s, costate[s + 1], moments - 1 + s)
    def forward(s, b, j):
        start = REACH if b < REACH else 5 * REACH - blocks
        at = pl.ds(pl.multiple_of((near[b, j] - anchor + start) * cols, cols), cols)
        return before[s, :, at]

    tail = slice((2 * moments - 1) * levels, (2 * moments - 1) * levels + ROW_TILE)
    one, two = first[tail, :cols].astype(F32), second[tail, :cols].astype(F32)
    left = jnp.where(odd == 1, one, two)
    right = jnp.where(odd == 1, two, one)

    def backward(s, n, j):
        total = None
        for b in range(n - REACH, n + REACH + 1):
            start = REACH if n < REACH else 5 * REACH - blocks
            source = after[s, :, (b + start) * cols : (b + start + 1) * cols]
            if 0 <= b < blocks:
                term = jnp.where(near[b, j] == anchor + n, source, jnp.zeros_like(source))
            else:
                row = b + blocks if b < 0 else b - blocks
                offset = (left if b < 0 else right)[row : row + 1, j : j + 1]
                hit = jnp.where(offset == float(n - b), 1.0, 0.0)
                term = source * jnp.broadcast_to(hit, source.shape).astype(BF16)
            total = term if total is None else total + term
        return total

    def ends(field, s):
        return jnp.concatenate([field[s, :, :width], field[s, :, cols_all - width :]], axis=1).astype(F32)

    def run_forward(which):
        for s, pushed in mixed(forward, which, outer, entries, pair_fwd, vert_fwd, stage):
            residual[s, :, :width] = (incr[s, :, :width].astype(F32) - pushed[:, :width]).astype(BF16)
            residual[s, :, width : cols_all - width] = inner_residual[s]
            residual[s, :, cols_all - width :] = (
                incr[s, :, cols_all - width :].astype(F32) - pushed[:, width:]
            ).astype(BF16)

    def run_backward(which):
        for s, value in mixed(backward, which, outer, entries, pair_bwd, vert_bwd, stage):
            base[s] = ends(costate, s) - value

    @pl.when(tm == 0)
    def _():
        residual[0] = incr[0]
        fill(after, moments - 1, crossed[...], 2 * (moments - 1))
        run_backward([moments - 1])

    @pl.when(tm == 1)
    def _():
        fill(before, 0, crossed[...], 2 * (moments - 1))
        run_forward([0])
        base[moments - 1] = ends(costate, moments - 1)

    run_forward(range(1, moments))
    copies = fetched([(residual.at[s], residual_any.at[s]) for s in range(moments)], sems)
    run_backward(range(moments - 1))
    for copy in copies:
        copy.wait()


def observe_kernel(packed, incr, arrived, target, inner_base, outer_base, adjoint_any, image, adjoint, masked, sems):
    moments, levels, cols_all = incr.shape
    slots = target.shape[1]
    width = outer_base.shape[2] // 2
    cols = width // REACH
    blocks = cols_all // cols
    inner_lanes = slice(width, cols_all - width)
    copies = []
    for s in range(moments):
        block = target[s : s + 1]
        if packed:
            cap = arrived.shape[2] // moments
            part = slice(s * cap, (s + 1) * cap)
            whole = jnp.concatenate([arrived[h, :, part] for h in range(arrived.shape[0])], axis=1)
        else:
            whole = arrived[s]
        lateral = whole[:cols]
        vertical = whole[cols : cols + levels].astype(F32)
        weight = whole[cols + levels : cols + levels + ROW_TILE].astype(F32)[:1]
        for b in range(blocks):
            hit = jnp.where(block == b, 1.0, 0.0)
            masked[s % 2, b * cols : (b + 1) * cols] = lateral * jnp.broadcast_to(hit, lateral.shape).astype(BF16)
        along = dot(incr[s], masked[s % 2])
        image[s : s + 1] = jnp.sum(vertical * along, axis=0, keepdims=True)
        push = dot_nt((vertical * weight).astype(BF16), masked[s % 2])
        adjoint[s, :, :width] = (outer_base[s, :, :width] + push[:, :width]).astype(BF16)
        adjoint[s, :, inner_lanes] = (inner_base[s] + push[:, inner_lanes]).astype(BF16)
        adjoint[s, :, cols_all - width :] = (outer_base[s, :, width:] + push[:, cols_all - width :]).astype(BF16)
        copies += fetched([(adjoint.at[s], adjoint_any.at[s])], sems.at[pl.ds(s, 1)])
    for copy in copies:
        copy.wait()


def on_device(
    incr, costate, lateral_mix, vertical_mix, neighbours,
    obs_lateral, obs_vertical, obs_weight, obs_block, obs_count,
):
    moments, levels, cols_all = incr.shape
    entries, cols, _ = lateral_mix.shape
    blocks = neighbours.shape[0]
    slots = obs_block.shape[1]
    tiles = lax.axis_size("space")
    cap = slots // tiles
    width = REACH * cols
    tm = lax.axis_index("tm")
    shape = jax.ShapeDtypeStruct
    semaphores = pltpu.SemaphoreType.DMA

    crossed = lax.ppermute(jnp.where(tm == 0, incr[-1], costate[0]), "tm", [(0, 1), (1, 0)])

    height = cols + levels + ROW_TILE
    packed = moments * cap == 128
    if packed:
        outgoing = call(
            pack_kernel,
            shape((tiles, height, moments * cap), BF16),
            (obs_lateral, obs_vertical, obs_weight),
            [ANY] * 3,
            scratch=[pltpu.VMEM(a.shape, BF16) for a in (obs_lateral, obs_vertical, obs_weight)] + [semaphores((3,))],
            cost=1,
        )
    else:
        stacked = jnp.concatenate(
            [obs_lateral, obs_vertical, jnp.broadcast_to(obs_weight[:, None], (moments, ROW_TILE, slots))], axis=1
        )
        outgoing = stacked.reshape(moments, height, tiles, cap).transpose(2, 1, 0, 3).reshape(tiles, height, -1)

    halo = shape(((2 * moments - 1) * levels + ROW_TILE, width), BF16)
    first, second = call(
        edges_kernel,
        [halo, halo],
        (neighbours, incr, costate, crossed),
        [ANY] * 4,
        scratch=[pltpu.VMEM(neighbours.shape, jnp.int32), semaphores, semaphores((4 * moments - 2,))],
        cost=1,
    )
    outgoing = gated(outgoing, first)
    first = exchanged(first, [(i, i + 1) for i in range(0, tiles - 1, 2)])
    second = exchanged(second, [(i, i + 1) for i in range(1, tiles - 1, 2)])
    arrived = lax.all_to_all(outgoing, "space", split_axis=0, concat_axis=0, tiled=True)
    if not packed:
        arrived = arrived.reshape(tiles, height, moments, cap).transpose(2, 1, 0, 3).reshape(moments, height, slots)

    pairs = (entries + 1) // 2
    inner = cols_all - 2 * width
    inner_residual, inner_base, *weights, target = call(
        interior_kernel,
        [shape((moments, levels, inner), BF16), shape((moments, levels, inner), F32)]
        + [shape((pairs, 2 * cols, 2 * cols), BF16)] * 2
        + [shape((levels, entries * levels), BF16)] * 2
        + [shape(obs_block.shape, jnp.int32)],
        (neighbours, obs_count, incr, costate, crossed, lateral_mix, vertical_mix, obs_block),
        [SMEM] * 2 + [VMEM] * 6,
        scratch=[pltpu.VMEM((moments, entries * levels, inner), BF16)],
        cost=4,
    )

    residual, outer_base = call(
        edge_kernel,
        [shape(incr.shape, BF16), shape((moments, levels, 2 * width), F32)],
        (neighbours, incr, costate, crossed, first, second, *weights, inner_residual),
        [SMEM] + [VMEM] * 10,
        out_specs=[HBM, VMEM],
        scratch=[pltpu.VMEM(incr.shape, BF16)]
        + [pltpu.VMEM((moments, levels, 6 * width), BF16)] * 2
        + [pltpu.VMEM((moments, entries * levels, 2 * width), BF16), semaphores((moments,))],
        cost=4,
    )

    adjoint, image = call(
        functools.partial(observe_kernel, packed),
        [shape(incr.shape, BF16), shape((moments, slots), F32)],
        (incr, arrived, target, inner_base, outer_base),
        [VMEM] * 5,
        out_specs=[HBM, VMEM],
        scratch=[pltpu.VMEM(incr.shape, BF16), pltpu.VMEM((2, cols_all, slots), BF16), semaphores((moments,))],
        cost=3,
    )
    return residual, adjoint, image


def solution(mesh):
    fields = P(("groups", "tm"), None, "space")
    rows = P(("groups", "tm"), "space")
    in_specs = (
        fields, fields, P(), P(), P(("groups", "space"), None), fields, fields, rows, rows, rows,
    )
    return jax.shard_map(
        on_device, mesh=mesh, in_specs=in_specs, out_specs=(fields, fields, rows), check_vma=False
    )
```

time: 37.9 us -> 31.2 us (0.82)
  the two profiles are of different devices: /device:TPU:9 before, /device:TPU:0 now
where the time goes in v1:
time: 31.2 us; the launch traced here: 30.9 us
  Pallas kernels  13.6 us (44%)
  starting transfers between devices  11.5 us (37%)
  waiting for transfers between devices  2.05 us (7%)
  local copies, waits for them, and re-layouts  1.89 us (6%)
  other arithmetic  1.03 us (3%)
  between operations  0.85 us (3%)
    pallas_call x6, Pallas kernels, call(): pl.pallas_call(kernel, out_shape=out_shape, in_specs=specs, out_specs=out...  13.6 us
    all_to_all x1, starting transfers between devices, on_device(): lax.all_to_all(outgoing, 'space', split_axis=0, concat_axis=0, tiled=True)  7.72 us
    ppermute x2, starting transfers between devices, exchanged(): return lax.ppermute(array, 'space', both)  3.25 us
    all_to_all x1, waiting for transfers between devices, on_device(): lax.all_to_all(outgoing, 'space', split_axis=0, concat_axis=0, tiled=True)  2.04 us
    unnamed x24, local copies, waits for them, and re-layouts  1.89 us
    select_n x1, other arithmetic, on_device(): jnp.where(tm == 0, incr[-1], costate[0])  1.03 us
  transfers between devices with their start and end apart: 4, of which 1 were waited for; matrix products, arithmetic and copies ran while one was open for 0% of the time, Pallas kernels for 35%

profile of v1, /device:TPU:0, one launch (start us, length us, event | category | flops | bytes accessed | tf_op | source)
XLA Modules:
  0.0 30.9 jit_solution(15409585690235941992)
XLA Ops:
  0.6 0.0 copy-start.3
  0.6 0.0 copy-start.5
  0.7 0.0 copy-start.8
  0.7 1.0 %select_bitcast_fusion = bf16[64,1024]{1,0:T(8,128)(2,1)S(1)} fusion(bf16[4,64,1024]{2,1,0:T(8,128)(2,1)} %costate.5, bf16[4,64,1024]{2,1,0:T(8,128)(2,1)} %incr.7, pred[]{:T(512)S(6)} %eq.3), kind=kLoop, calls=%fused_computation | loop fusion | flops 65536 | bytes 393217 | tf_op jit(solution)/shard_map/jit(_where)/select_n | solution.py:328
  1.7 0.0 copy-start
  1.7 0.0 copy-start.1
  1.7 0.0 copy-start.7
  1.7 0.5 %collective-permute-start = (bf16[64,1024]{1,0:T(8,128)(2,1)S(1)}, bf16[64,1024]{1,0:T(8,128)(2,1)S(1)}, u32[]{:S(2)}, u32[]{:S(2)}) collective-permute-start(bf16[64,1024]{1,0:T(8,128)(2,1)S(1)} %select_bitcast_fusion), channel_id=1, source_target_pairs={{0,1},{1,0},{2,3},{3,2},{4,5},{5,4},{6,7},{7,6},{8,9},{9,8},{10,11... | collective-permute-start | bytes 393224 | tf_op jit(solution)/shard_map/ppermute | solution.py:328
  2.3 0.0 copy-done.3
  2.3 0.0 copy-done.5
  2.3 0.0 copy-done.8
  2.3 1.4 %shard_map.124.data = bf16[8,208,128]{2,1,0:T(8,128)(2,1)} custom-call(bf16[4,128,256]{2,1,0:T(8,128)(2,1)S(1)} %copy-done.3, bf16[4,64,256]{2,1,0:T(8,128)(2,1)S(1)} %copy-done.5, bf16[4,256]{1,0:T(4,128)(2,1)S(1)} %copy-done.8), custom_call_target="tpu_custom_call" | custom-call | flops 1000000000 | bytes 1000000 | tf_op jit(solution)/shard_map/pallas_call | solution.py:36
  3.6 0.0 collective-permute-done.crossed
  3.7 0.0 copy-done
  3.7 0.0 copy-done.1
  3.7 0.0 copy-done.7
  3.7 0.3 shard_map.121
  4.0 2.6 %collective-permute-start.1 = (bf16[464,256]{1,0:T(8,128)(2,1)S(1)}, bf16[464,256]{1,0:T(8,128)(2,1)S(1)}, u32[]{:S(2)}, u32[]{:S(2)}) collective-permute-start(bf16[464,256]{1,0:T(8,128)(2,1)S(1)} %get-tuple-element.16.after), channel_id=1, source_target_pairs={{0,2},{4,6},{8,10},{12,14},{2,0},{6,4},{10,8},{14,12},{1,3},{5,7},... | collective-permute-start | bytes 712712 | tf_op jit(solution)/shard_map/ppermute | solution.py:31
  6.6 0.7 %collective-permute-start.2 = (bf16[464,256]{1,0:T(8,128)(2,1)S(1)}, bf16[464,256]{1,0:T(8,128)(2,1)S(1)}, u32[]{:S(2)}, u32[]{:S(2)}) collective-permute-start(bf16[464,256]{1,0:T(8,128)(2,1)S(1)} %get-tuple-element.17), channel_id=1, source_target_pairs={{2,4},{6,8},{10,12},{4,2},{8,6},{12,10},{3,5},{7,9},{11,13},{5,3},... | collective-permute-start | bytes 712712 | tf_op jit(solution)/shard_map/ppermute | solution.py:31
  7.2 0.0 copy-start.2
  7.3 0.0 copy-start.4
  7.3 0.0 copy-start.6
  7.3 0.0 copy-start.9
  7.3 7.7 %all-to-all-start = ((bf16[8,208,128]{2,1,0:T(8,128)(2,1)}), bf16[8,208,128]{2,1,0:T(8,128)(2,1)S(1)}, u32[]{:S(2)}, u32[]{:S(2)}) async-start(bf16[8,208,128]{2,1,0:T(8,128)(2,1)} %shard_map.125), calls=%async_computation | async-start | bytes 851968 | tf_op jit(solution)/shard_map/all_to_all | solution.py:359
  15.0 0.0 copy-done.2
  15.0 0.0 copy-done.4
  15.0 0.0 copy-done.6
  15.0 0.0 copy-done.9
  15.0 4.6 %shard_map.122 = (bf16[4,64,512]{2,1,0:T(8,128)(2,1)S(1)}, f32[4,64,512]{2,1,0:T(8,128)S(1)}, bf16[5,256,256]{2,1,0:T(8,128)(2,1)S(1)}, bf16[5,256,256]{2,1,0:T(...) custom-call(s32[8,9]{1,0:T(8,128)S(1)} %copy-done.7, ...), custom_call_target="tpu_custom_call" | custom-call | flops 4000000000 | bytes 4000000 | tf_op jit(solution)/shard_map/pallas_call | solution.py:36
  19.7 0.0 collective-permute-done.1.first
  19.7 0.0 collective-permute-done.2.second
  19.7 4.9 %shard_map.123 = (bf16[4,64,1024]{2,1,0:T(8,128)(2,1)}, f32[4,64,512]{2,1,0:T(8,128)S(1)}) custom-call(s32[8,9]{1,0:T(8,128)S(1)} %copy-done.7, bf16[4,64,1024]{2,1,0:T(8,128)(2,1)S(1)} %copy-done.1, bf16[4,64,1024]{2,1,0:T(8,128)(2,1)S(1)} %copy-done, bf16[64,1024]{1,0:T(8,128)(2,1)S(1)} %collective-permute-done.crossed, ...), custom_call_target="tpu_custom_call" | custom-call | flops 4000000000 | bytes 4000000 | tf_op jit(solution)/shard_map/pallas_call | solution.py:36
  24.6 0.0 copy-start.10
  24.6 0.8 %copy-done.10 = f32[4,64,512]{2,1,0:T(8,128)} copy-done((f32[4,64,512]{2,1,0:T(8,128)}, f32[4,64,512]{2,1,0:T(8,128)S(1)}, u32[]{:S(2)}) %copy-start.10) | copy-done | bytes 524312
  25.4 2.0 %all-to-all-done.arrived = bf16[8,208,128]{2,1,0:T(8,128)(2,1)S(1)} async-done(((bf16[8,208,128]{2,1,0:T(8,128)(2,1)}), bf16[8,208,128]{2,1,0:T(8,128)(2,1)S(1)}, u32[]{:S(2)}, u32[]{:S(2)}) %all-to-all-start) | async-done | bytes 426016 | tf_op jit(solution)/shard_map/all_to_all | solution.py:359
  27.5 0.0 copy-start.11
  27.5 1.0 %copy-done.11 = f32[4,64,512]{2,1,0:T(8,128)S(1)} copy-done((f32[4,64,512]{2,1,0:T(8,128)S(1)}, f32[4,64,512]{2,1,0:T(8,128)}, u32[]{:S(2)}) %copy-start.11) | copy-done | bytes 524312
  28.5 2.4 %shard_map.126 = (bf16[4,64,1024]{2,1,0:T(8,128)(2,1)}, f32[4,256]{1,0:T(4,128)}) custom-call(bf16[4,64,1024]{2,1,0:T(8,128)(2,1)S(1)} %copy-done.1, bf16[8,208,128]{2,1,0:T(8,128)(2,1)S(1)} %all-to-all-done.arrived, s32[4,256]{1,0:T(4,128)S(1)} %get-tuple-element.24.target, f32[4,64,512]{2,1,0:T(8,128)S(1)} %get-tuple-element.25.inner_base, ...), custom_call_target="tpu_custom_call" | custom-call | flops 3000000000 | bytes 3000000 | tf_op jit(solution)/shard_map/pallas_call | solution.py:36
  (1 shorter events, 0.0 us)
Async XLA Ops:
  0.6 1.6 %copy-start.3 = (bf16[4,128,256]{2,1,0:T(8,128)(2,1)S(1)}, bf16[4,128,256]{2,1,0:T(8,128)(2,1)}, u32[]{:S(2)}) copy-start(bf16[4,128,256]{2,1,0:T(8,128)(2,1)} %lateral_any.1) | copy-start | bytes 786436
  0.6 1.6 %copy-start.5 = (bf16[4,64,256]{2,1,0:T(8,128)(2,1)S(1)}, bf16[4,64,256]{2,1,0:T(8,128)(2,1)}, u32[]{:S(2)}) copy-start(bf16[4,64,256]{2,1,0:T(8,128)(2,1)} %vertical_any.1) | copy-start | bytes 393220
  0.7 1.6 %copy-start.8 = (bf16[4,256]{1,0:T(4,128)(2,1)S(1)}, bf16[4,256]{1,0:T(4,128)(2,1)}, u32[]{:S(2)}) copy-start(bf16[4,256]{1,0:T(4,128)(2,1)} %weight_any.1) | copy-start | bytes 6148
  1.7 2.0 %copy-start = (bf16[4,64,1024]{2,1,0:T(8,128)(2,1)S(1)}, bf16[4,64,1024]{2,1,0:T(8,128)(2,1)}, u32[]{:S(2)}) copy-start(bf16[4,64,1024]{2,1,0:T(8,128)(2,1)} %costate.5) | copy-start | bytes 1572868
  1.7 2.0 %copy-start.1 = (bf16[4,64,1024]{2,1,0:T(8,128)(2,1)S(1)}, bf16[4,64,1024]{2,1,0:T(8,128)(2,1)}, u32[]{:S(2)}) copy-start(bf16[4,64,1024]{2,1,0:T(8,128)(2,1)} %incr.7) | copy-start | bytes 1572868
  1.7 2.0 %copy-start.7 = (s32[8,9]{1,0:T(8,128)S(1)}, s32[8,9]{1,0:T(8,128)}, u32[]{:S(2)}) copy-start(s32[8,9]{1,0:T(8,128)} %near.3) | copy-start | bytes 868
  1.7 1.9 %collective-permute-start = (bf16[64,1024]{1,0:T(8,128)(2,1)S(1)}, bf16[64,1024]{1,0:T(8,128)(2,1)S(1)}, u32[]{:S(2)}, u32[]{:S(2)}) collective-permute-start(bf16[64,1024]{1,0:T(8,128)(2,1)S(1)} %select_bitcast_fusion), channel_id=1, source_target_pairs={{0,1},{1,0},{2,3},{3,2},{4,5},{5,4},{6,7},{7,6},{8,9},{9,8},{10,11... | collective-permute-start | bytes 393224 | tf_op jit(solution)/shard_map/ppermute | solution.py:328
  4.0 15.7 %collective-permute-start.1 = (bf16[464,256]{1,0:T(8,128)(2,1)S(1)}, bf16[464,256]{1,0:T(8,128)(2,1)S(1)}, u32[]{:S(2)}, u32[]{:S(2)}) collective-permute-start(bf16[464,256]{1,0:T(8,128)(2,1)S(1)} %get-tuple-element.16.after), channel_id=1, source_target_pairs={{0,2},{4,6},{8,10},{12,14},{2,0},{6,4},{10,8},{14,12},{1,3},{5,7},... | collective-permute-start | bytes 712712 | tf_op jit(solution)/shard_map/ppermute | solution.py:31
  6.6 13.1 %collective-permute-start.2 = (bf16[464,256]{1,0:T(8,128)(2,1)S(1)}, bf16[464,256]{1,0:T(8,128)(2,1)S(1)}, u32[]{:S(2)}, u32[]{:S(2)}) collective-permute-start(bf16[464,256]{1,0:T(8,128)(2,1)S(1)} %get-tuple-element.17), channel_id=1, source_target_pairs={{2,4},{6,8},{10,12},{4,2},{8,6},{12,10},{3,5},{7,9},{11,13},{5,3},... | collective-permute-start | bytes 712712 | tf_op jit(solution)/shard_map/ppermute | solution.py:31
  7.2 7.8 %copy-start.2 = (bf16[9,128,128]{2,1,0:T(8,128)(2,1)S(1)}, bf16[9,128,128]{2,1,0:T(8,128)(2,1)}, u32[]{:S(2)}) copy-start(bf16[9,128,128]{2,1,0:T(8,128)(2,1)} %lateral_mix.1) | copy-start | bytes 884740
  7.3 7.8 %copy-start.4 = (bf16[9,64,64]{2,1,0:T(8,128)(2,1)S(1)}, bf16[9,64,64]{2,1,0:T(8,128)(2,1)}, u32[]{:S(2)}) copy-start(bf16[9,64,64]{2,1,0:T(8,128)(2,1)} %vertical_mix.1) | copy-start | bytes 221188
  7.3 7.8 %copy-start.6 = (s32[4,256]{1,0:T(4,128)S(1)}, s32[4,256]{1,0:T(4,128)}, u32[]{:S(2)}) copy-start(s32[4,256]{1,0:T(4,128)} %owner.1) | copy-start | bytes 12292
  7.3 7.8 %copy-start.9 = (s32[4,8]{1,0:T(4,128)S(1)}, s32[4,8]{1,0:T(4,128)}, u32[]{:S(2)}) copy-start(s32[4,8]{1,0:T(4,128)} %counts.1) | copy-start | bytes 388
  7.3 20.2 %all-to-all-start = ((bf16[8,208,128]{2,1,0:T(8,128)(2,1)}), bf16[8,208,128]{2,1,0:T(8,128)(2,1)S(1)}, u32[]{:S(2)}, u32[]{:S(2)}) async-start(bf16[8,208,128]{2,1,0:T(8,128)(2,1)} %shard_map.125), calls=%async_computation | async-start | bytes 851968 | tf_op jit(solution)/shard_map/all_to_all | solution.py:359
  24.6 0.8 %copy-start.10 = (f32[4,64,512]{2,1,0:T(8,128)}, f32[4,64,512]{2,1,0:T(8,128)S(1)}, u32[]{:S(2)}) copy-start(f32[4,64,512]{2,1,0:T(8,128)S(1)} %get-tuple-element.26.outer_base) | copy-start | bytes 1572868
  27.5 1.0 %copy-start.11 = (f32[4,64,512]{2,1,0:T(8,128)S(1)}, f32[4,64,512]{2,1,0:T(8,128)}, u32[]{:S(2)}) copy-start(f32[4,64,512]{2,1,0:T(8,128)} %copy-done.10) | copy-start | bytes 1572868

commit v2 on v1

--- a/solution.py
+++ b/solution.py
@@ -8,7 +8,7 @@
 from jax.sharding import PartitionSpec as P
 
 REACH = 2
-ROW_TILE = 16
+ROWS = 8
 FULL = 63.6
 BF16 = jnp.bfloat16
 F32 = jnp.float32
@@ -73,9 +73,9 @@
     fetch.wait()
     own = lax.broadcasted_iota(jnp.int32, near.shape, 0) + place * blocks
     distance = (near[...] - own).astype(F32)
-    distance = jnp.concatenate([distance, jnp.zeros((ROW_TILE - blocks, entries), F32)], axis=0).astype(BF16)
+    distance = distance.astype(BF16)
     for target in (first, second):
-        target[len(slabs) * levels :] = jnp.zeros((ROW_TILE, width), BF16)
+        target[len(slabs) * levels :] = jnp.zeros((ROWS, width), BF16)
         target[len(slabs) * levels :, :entries] = distance
     for copy in copies:
         copy.wait()
@@ -98,7 +98,7 @@
             [obs_vertical[s, :, lanes] for s in range(moments)], axis=1
         )
         row = jnp.concatenate([obs_weight[s : s + 1, lanes].astype(F32) for s in range(moments)], axis=1)
-        out[tile, cols + levels :] = jnp.broadcast_to(row, (ROW_TILE, row.shape[1])).astype(BF16)
+        out[tile, cols + levels :] = jnp.broadcast_to(row, (ROWS, row.shape[1])).astype(BF16)
 
 
 def gate_kernel(data, after, out):
@@ -194,9 +194,11 @@
 
 def edge_kernel(
     near, incr, costate, crossed, first, second, pair_fwd, pair_bwd, vert_fwd, vert_bwd, inner_residual,
-    residual_any, base, residual, before, after, stage, sems,
+    residual_any, *rest,
 ):
     moments, levels, cols_all = incr.shape
+    base = rest[:moments]
+    residual, before, after, stage, sems = rest[moments:]
     blocks, entries = near.shape
     cols = cols_all // blocks
     width = REACH * cols
@@ -223,7 +225,7 @@
         at = pl.ds(pl.multiple_of((near[b, j] - anchor + start) * cols, cols), cols)
         return before[s, :, at]
 
-    tail = slice((2 * moments - 1) * levels, (2 * moments - 1) * levels + ROW_TILE)
+    tail = slice((2 * moments - 1) * levels, (2 * moments - 1) * levels + ROWS)
     one, two = first[tail, :cols].astype(F32), second[tail, :cols].astype(F32)
     left = jnp.where(odd == 1, one, two)
     right = jnp.where(odd == 1, two, one)
@@ -256,7 +258,7 @@
 
     def run_backward(which):
         for s, value in mixed(backward, which, outer, entries, pair_bwd, vert_bwd, stage):
-            base[s] = ends(costate, s) - value
+            base[s][...] = ends(costate, s) - value
 
     @pl.when(tm == 0)
     def _():
@@ -268,7 +270,7 @@
     def _():
         fill(before, 0, crossed[...], 2 * (moments - 1))
         run_forward([0])
-        base[moments - 1] = ends(costate, moments - 1)
+        base[moments - 1][...] = ends(costate, moments - 1)
 
     run_forward(range(1, moments))
     copies = fetched([(residual.at[s], residual_any.at[s]) for s in range(moments)], sems)
@@ -277,10 +279,12 @@
         copy.wait()
 
 
-def observe_kernel(packed, incr, arrived, target, inner_base, outer_base, adjoint_any, image, adjoint, masked, sems):
+def observe_kernel(packed, incr, arrived, target, inner_base, *rest):
     moments, levels, cols_all = incr.shape
+    outer_base = rest[:moments]
+    adjoint_any, image, adjoint, masked, sems = rest[moments:]
     slots = target.shape[1]
-    width = outer_base.shape[2] // 2
+    width = outer_base[0].shape[1] // 2
     cols = width // REACH
     blocks = cols_all // cols
     inner_lanes = slice(width, cols_all - width)
@@ -295,16 +299,16 @@
             whole = arrived[s]
         lateral = whole[:cols]
         vertical = whole[cols : cols + levels].astype(F32)
-        weight = whole[cols + levels : cols + levels + ROW_TILE].astype(F32)[:1]
+        weight = whole[cols + levels : cols + levels + ROWS].astype(F32)[:1]
         for b in range(blocks):
             hit = jnp.where(block == b, 1.0, 0.0)
             masked[s % 2, b * cols : (b + 1) * cols] = lateral * jnp.broadcast_to(hit, lateral.shape).astype(BF16)
         along = dot(incr[s], masked[s % 2])
         image[s : s + 1] = jnp.sum(vertical * along, axis=0, keepdims=True)
         push = dot_nt((vertical * weight).astype(BF16), masked[s % 2])
-        adjoint[s, :, :width] = (outer_base[s, :, :width] + push[:, :width]).astype(BF16)
+        adjoint[s, :, :width] = (outer_base[s][:, :width] + push[:, :width]).astype(BF16)
         adjoint[s, :, inner_lanes] = (inner_base[s] + push[:, inner_lanes]).astype(BF16)
-        adjoint[s, :, cols_all - width :] = (outer_base[s, :, width:] + push[:, cols_all - width :]).astype(BF16)
+        adjoint[s, :, cols_all - width :] = (outer_base[s][:, width:] + push[:, cols_all - width :]).astype(BF16)
         copies += fetched([(adjoint.at[s], adjoint_any.at[s])], sems.at[pl.ds(s, 1)])
     for copy in copies:
         copy.wait()
@@ -327,7 +331,7 @@
 
     crossed = lax.ppermute(jnp.where(tm == 0, incr[-1], costate[0]), "tm", [(0, 1), (1, 0)])
 
-    height = cols + levels + ROW_TILE
+    height = cols + levels + ROWS
     packed = moments * cap == 128
     if packed:
         outgoing = call(
@@ -340,11 +344,11 @@
         )
     else:
         stacked = jnp.concatenate(
-            [obs_lateral, obs_vertical, jnp.broadcast_to(obs_weight[:, None], (moments, ROW_TILE, slots))], axis=1
+            [obs_lateral, obs_vertical, jnp.broadcast_to(obs_weight[:, None], (moments, ROWS, slots))], axis=1
         )
         outgoing = stacked.reshape(moments, height, tiles, cap).transpose(2, 1, 0, 3).reshape(tiles, height, -1)
 
-    halo = shape(((2 * moments - 1) * levels + ROW_TILE, width), BF16)
+    halo = shape(((2 * moments - 1) * levels + ROWS, width), BF16)
     first, second = call(
         edges_kernel,
         [halo, halo],
@@ -374,12 +378,12 @@
         cost=4,
     )
 
-    residual, outer_base = call(
+    residual, *outer_base = call(
         edge_kernel,
-        [shape(incr.shape, BF16), shape((moments, levels, 2 * width), F32)],
+        [shape(incr.shape, BF16)] + [shape((levels, 2 * width), F32)] * moments,
         (neighbours, incr, costate, crossed, first, second, *weights, inner_residual),
         [SMEM] + [VMEM] * 10,
-        out_specs=[HBM, VMEM],
+        out_specs=[HBM] + [VMEM] * moments,
         scratch=[pltpu.VMEM(incr.shape, BF16)]
         + [pltpu.VMEM((moments, levels, 6 * width), BF16)] * 2
         + [pltpu.VMEM((moments, entries * levels, 2 * width), BF16), semaphores((moments,))],
@@ -389,8 +393,8 @@
     adjoint, image = call(
         functools.partial(observe_kernel, packed),
         [shape(incr.shape, BF16), shape((moments, slots), F32)],
-        (incr, arrived, target, inner_base, outer_base),
-        [VMEM] * 5,
+        (incr, arrived, target, inner_base, *outer_base),
+        [VMEM] * (4 + moments),
         out_specs=[HBM, VMEM],
         scratch=[pltpu.VMEM(incr.shape, BF16), pltpu.VMEM((2, cols_all, slots), BF16), semaphores((moments,))],
         cost=3,

time: 31.2 us -> 29.8 us (0.955)
  local copies, waits for them, and re-layouts: 1.89 us -> 0.06 us
  waiting for transfers between devices: 2.05 us -> 2.49 us
    unnamed x24 -> x20, local copies, waits for them, and re-layouts: 1.89 us -> 0.06 us
    all_to_all x1, waiting for transfers between devices: 2.04 us -> 2.48 us  [on_device(): lax.all_to_all(outgoing, 'space', split_axis=0, concat_axis=0, tiled=True)]
  transfers between devices with their start and end apart: 4 -> 4, of which waited for: 1 -> 1; matrix products, arithmetic and copies ran while one was open for 0% -> 0% of each run, Pallas kernels for 35% -> 37%
where the time goes in v2:
time: 29.8 us; the launch traced here: 29.5 us
  Pallas kernels  13.6 us (46%)
  starting transfers between devices  11.5 us (39%)
  waiting for transfers between devices  2.49 us (8%)
  other arithmetic  1.03 us (3%)
  between operations  0.84 us (3%)
    pallas_call x6, Pallas kernels, call(): pl.pallas_call(kernel, out_shape=out_shape, in_specs=specs, out_specs=out...  13.6 us
    all_to_all x1, starting transfers between devices, on_device(): lax.all_to_all(outgoing, 'space', split_axis=0, concat_axis=0, tiled=True)  7.72 us
    ppermute x2, starting transfers between devices, exchanged(): return lax.ppermute(array, 'space', both)  3.25 us
    all_to_all x1, waiting for transfers between devices, on_device(): lax.all_to_all(outgoing, 'space', split_axis=0, concat_axis=0, tiled=True)  2.48 us
    select_n x1, other arithmetic, on_device(): jnp.where(tm == 0, incr[-1], costate[0])  1.03 us
  transfers between devices with their start and end apart: 4, of which 1 were waited for; matrix products, arithmetic and copies ran while one was open for 0% of the time, Pallas kernels for 37%

profile of v2, /device:TPU:0, one launch (start us, length us, event | category | flops | bytes accessed | tf_op | source)
XLA Modules:
  0.0 29.5 jit_solution(3123593467370033561)
XLA Ops:
  0.6 0.0 copy-start.3
  0.6 0.0 copy-start.5
  0.7 0.0 copy-start.8
  0.7 1.0 %select_bitcast_fusion = bf16[64,1024]{1,0:T(8,128)(2,1)S(1)} fusion(bf16[4,64,1024]{2,1,0:T(8,128)(2,1)} %costate.5, bf16[4,64,1024]{2,1,0:T(8,128)(2,1)} %incr.7, pred[]{:T(512)S(6)} %eq.3), kind=kLoop, calls=%fused_computation | loop fusion | flops 65536 | bytes 393217 | tf_op jit(solution)/shard_map/jit(_where)/select_n | solution.py:332
  1.7 0.0 copy-start
  1.7 0.0 copy-start.1
  1.7 0.0 copy-start.7
  1.7 0.5 %collective-permute-start = (bf16[64,1024]{1,0:T(8,128)(2,1)S(1)}, bf16[64,1024]{1,0:T(8,128)(2,1)S(1)}, u32[]{:S(2)}, u32[]{:S(2)}) collective-permute-start(bf16[64,1024]{1,0:T(8,128)(2,1)S(1)} %select_bitcast_fusion), channel_id=1, source_target_pairs={{0,1},{1,0},{2,3},{3,2},{4,5},{5,4},{6,7},{7,6},{8,9},{9,8},{10,11... | collective-permute-start | bytes 393224 | tf_op jit(solution)/shard_map/ppermute | solution.py:332
  2.3 0.0 copy-done.3
  2.3 0.0 copy-done.5
  2.3 0.0 copy-done.8
  2.3 1.4 %shard_map.124.data = bf16[8,200,128]{2,1,0:T(8,128)(2,1)} custom-call(bf16[4,128,256]{2,1,0:T(8,128)(2,1)S(1)} %copy-done.3, bf16[4,64,256]{2,1,0:T(8,128)(2,1)S(1)} %copy-done.5, bf16[4,256]{1,0:T(4,128)(2,1)S(1)} %copy-done.8), custom_call_target="tpu_custom_call" | custom-call | flops 1000000000 | bytes 1000000 | tf_op jit(solution)/shard_map/pallas_call | solution.py:36
  3.6 0.0 collective-permute-done.crossed
  3.6 0.0 copy-done
  3.7 0.0 copy-done.1
  3.7 0.0 copy-done.7
  3.7 0.3 shard_map.121
  4.0 2.6 %collective-permute-start.1 = (bf16[456,256]{1,0:T(8,128)(2,1)S(1)}, bf16[456,256]{1,0:T(8,128)(2,1)S(1)}, u32[]{:S(2)}, u32[]{:S(2)}) collective-permute-start(bf16[456,256]{1,0:T(8,128)(2,1)S(1)} %get-tuple-element.19.after), channel_id=1, source_target_pairs={{0,2},{4,6},{8,10},{12,14},{2,0},{6,4},{10,8},{14,12},{1,3},{5,7},... | collective-permute-start | bytes 700424 | tf_op jit(solution)/shard_map/ppermute | solution.py:31
  6.5 0.7 %collective-permute-start.2 = (bf16[456,256]{1,0:T(8,128)(2,1)S(1)}, bf16[456,256]{1,0:T(8,128)(2,1)S(1)}, u32[]{:S(2)}, u32[]{:S(2)}) collective-permute-start(bf16[456,256]{1,0:T(8,128)(2,1)S(1)} %get-tuple-element.20), channel_id=1, source_target_pairs={{2,4},{6,8},{10,12},{4,2},{8,6},{12,10},{3,5},{7,9},{11,13},{5,3},... | collective-permute-start | bytes 700424 | tf_op jit(solution)/shard_map/ppermute | solution.py:31
  7.2 0.0 copy-start.2
  7.2 0.0 copy-start.4
  7.3 0.0 copy-start.6
  7.3 0.0 copy-start.9
  7.3 7.7 %all-to-all-start = ((bf16[8,200,128]{2,1,0:T(8,128)(2,1)}), bf16[8,200,128]{2,1,0:T(8,128)(2,1)S(1)}, u32[]{:S(2)}, u32[]{:S(2)}) async-start(bf16[8,200,128]{2,1,0:T(8,128)(2,1)} %shard_map.125), calls=%async_computation | async-start | bytes 819200 | tf_op jit(solution)/shard_map/all_to_all | solution.py:363
  15.0 0.0 copy-done.2
  15.0 0.0 copy-done.4
  15.0 0.0 copy-done.6
  15.0 0.0 copy-done.9
  15.0 4.6 %shard_map.122 = (bf16[4,64,512]{2,1,0:T(8,128)(2,1)S(1)}, f32[4,64,512]{2,1,0:T(8,128)S(1)}, bf16[5,256,256]{2,1,0:T(8,128)(2,1)S(1)}, bf16[5,256,256]{2,1,0:T(...) custom-call(s32[8,9]{1,0:T(8,128)S(1)} %copy-done.7, ...), custom_call_target="tpu_custom_call" | custom-call | flops 4000000000 | bytes 4000000 | tf_op jit(solution)/shard_map/pallas_call | solution.py:36
  19.7 0.0 collective-permute-done.1.first
  19.7 0.0 collective-permute-done.2.second
  19.7 4.9 %shard_map.123 = (bf16[4,64,1024]{2,1,0:T(8,128)(2,1)}, f32[64,512]{1,0:T(8,128)S(1)}, f32[64,512]{1,0:T(8,128)S(1)}, f32[64,512]{1,0:T(8,128)S(1)}, f32[64,512]{1,0:T(8,128)S(1)}) custom-call(s32[8,9]{1,0:T(8,128)S(1)} %copy-done.7, bf16[4,64,1024]{2,1,0:T(8,128)(2,1)S(1)} %copy-done.1, bf16[4,64,1024]{2,1,0:T(8,128)(2,1)S(1)} %copy-done, ...), custom_call_target="tpu_custom_call" | custom-call | flops 4000000000 | bytes 4000000 | tf_op jit(solution)/shard_map/pallas_call | solution.py:36
  24.6 2.5 %all-to-all-done.arrived = bf16[8,200,128]{2,1,0:T(8,128)(2,1)S(1)} async-done(((bf16[8,200,128]{2,1,0:T(8,128)(2,1)}), bf16[8,200,128]{2,1,0:T(8,128)(2,1)S(1)}, u32[]{:S(2)}, u32[]{:S(2)}) %all-to-all-start) | async-done | bytes 409632 | tf_op jit(solution)/shard_map/all_to_all | solution.py:363
  27.1 2.4 %shard_map.126 = (bf16[4,64,1024]{2,1,0:T(8,128)(2,1)}, f32[4,256]{1,0:T(4,128)}) custom-call(bf16[4,64,1024]{2,1,0:T(8,128)(2,1)S(1)} %copy-done.1, bf16[8,200,128]{2,1,0:T(8,128)(2,1)S(1)} %all-to-all-done.arrived, s32[4,256]{1,0:T(4,128)S(1)} %get-tuple-element.27.target, f32[4,64,512]{2,1,0:T(8,128)S(1)} %get-tuple-element.28.inner_base, ...), custom_call_target="tpu_custom_call" | custom-call | flops 3000000000 | bytes 3000000 | tf_op jit(solution)/shard_map/pallas_call | solution.py:36
  (1 shorter events, 0.0 us)
Async XLA Ops:
  0.6 1.6 %copy-start.3 = (bf16[4,128,256]{2,1,0:T(8,128)(2,1)S(1)}, bf16[4,128,256]{2,1,0:T(8,128)(2,1)}, u32[]{:S(2)}) copy-start(bf16[4,128,256]{2,1,0:T(8,128)(2,1)} %lateral_any.1) | copy-start | bytes 786436
  0.6 1.6 %copy-start.5 = (bf16[4,64,256]{2,1,0:T(8,128)(2,1)S(1)}, bf16[4,64,256]{2,1,0:T(8,128)(2,1)}, u32[]{:S(2)}) copy-start(bf16[4,64,256]{2,1,0:T(8,128)(2,1)} %vertical_any.1) | copy-start | bytes 393220
  0.7 1.6 %copy-start.8 = (bf16[4,256]{1,0:T(4,128)(2,1)S(1)}, bf16[4,256]{1,0:T(4,128)(2,1)}, u32[]{:S(2)}) copy-start(bf16[4,256]{1,0:T(4,128)(2,1)} %weight_any.1) | copy-start | bytes 6148
  1.7 1.9 %copy-start = (bf16[4,64,1024]{2,1,0:T(8,128)(2,1)S(1)}, bf16[4,64,1024]{2,1,0:T(8,128)(2,1)}, u32[]{:S(2)}) copy-start(bf16[4,64,1024]{2,1,0:T(8,128)(2,1)} %costate.5) | copy-start | bytes 1572868
  1.7 1.9 %copy-start.1 = (bf16[4,64,1024]{2,1,0:T(8,128)(2,1)S(1)}, bf16[4,64,1024]{2,1,0:T(8,128)(2,1)}, u32[]{:S(2)}) copy-start(bf16[4,64,1024]{2,1,0:T(8,128)(2,1)} %incr.7) | copy-start | bytes 1572868
  1.7 1.9 %copy-start.7 = (s32[8,9]{1,0:T(8,128)S(1)}, s32[8,9]{1,0:T(8,128)}, u32[]{:S(2)}) copy-start(s32[8,9]{1,0:T(8,128)} %near.3) | copy-start | bytes 868
  1.7 1.9 %collective-permute-start = (bf16[64,1024]{1,0:T(8,128)(2,1)S(1)}, bf16[64,1024]{1,0:T(8,128)(2,1)S(1)}, u32[]{:S(2)}, u32[]{:S(2)}) collective-permute-start(bf16[64,1024]{1,0:T(8,128)(2,1)S(1)} %select_bitcast_fusion), channel_id=1, source_target_pairs={{0,1},{1,0},{2,3},{3,2},{4,5},{5,4},{6,7},{7,6},{8,9},{9,8},{10,11... | collective-permute-start | bytes 393224 | tf_op jit(solution)/shard_map/ppermute | solution.py:332
  4.0 15.7 %collective-permute-start.1 = (bf16[456,256]{1,0:T(8,128)(2,1)S(1)}, bf16[456,256]{1,0:T(8,128)(2,1)S(1)}, u32[]{:S(2)}, u32[]{:S(2)}) collective-permute-start(bf16[456,256]{1,0:T(8,128)(2,1)S(1)} %get-tuple-element.19.after), channel_id=1, source_target_pairs={{0,2},{4,6},{8,10},{12,14},{2,0},{6,4},{10,8},{14,12},{1,3},{5,7},... | collective-permute-start | bytes 700424 | tf_op jit(solution)/shard_map/ppermute | solution.py:31
  6.5 13.1 %collective-permute-start.2 = (bf16[456,256]{1,0:T(8,128)(2,1)S(1)}, bf16[456,256]{1,0:T(8,128)(2,1)S(1)}, u32[]{:S(2)}, u32[]{:S(2)}) collective-permute-start(bf16[456,256]{1,0:T(8,128)(2,1)S(1)} %get-tuple-element.20), channel_id=1, source_target_pairs={{2,4},{6,8},{10,12},{4,2},{8,6},{12,10},{3,5},{7,9},{11,13},{5,3},... | collective-permute-start | bytes 700424 | tf_op jit(solution)/shard_map/ppermute | solution.py:31
  7.2 7.8 %copy-start.2 = (bf16[9,128,128]{2,1,0:T(8,128)(2,1)S(1)}, bf16[9,128,128]{2,1,0:T(8,128)(2,1)}, u32[]{:S(2)}) copy-start(bf16[9,128,128]{2,1,0:T(8,128)(2,1)} %lateral_mix.1) | copy-start | bytes 884740
  7.2 7.8 %copy-start.4 = (bf16[9,64,64]{2,1,0:T(8,128)(2,1)S(1)}, bf16[9,64,64]{2,1,0:T(8,128)(2,1)}, u32[]{:S(2)}) copy-start(bf16[9,64,64]{2,1,0:T(8,128)(2,1)} %vertical_mix.1) | copy-start | bytes 221188
  7.3 7.8 %copy-start.6 = (s32[4,256]{1,0:T(4,128)S(1)}, s32[4,256]{1,0:T(4,128)}, u32[]{:S(2)}) copy-start(s32[4,256]{1,0:T(4,128)} %owner.1) | copy-start | bytes 12292
  7.3 7.8 %copy-start.9 = (s32[4,8]{1,0:T(4,128)S(1)}, s32[4,8]{1,0:T(4,128)}, u32[]{:S(2)}) copy-start(s32[4,8]{1,0:T(4,128)} %counts.1) | copy-start | bytes 388
  7.3 19.8 %all-to-all-start = ((bf16[8,200,128]{2,1,0:T(8,128)(2,1)}), bf16[8,200,128]{2,1,0:T(8,128)(2,1)S(1)}, u32[]{:S(2)}, u32[]{:S(2)}) async-start(bf16[8,200,128]{2,1,0:T(8,128)(2,1)} %shard_map.125), calls=%async_computation | async-start | bytes 819200 | tf_op jit(solution)/shard_map/all_to_all | solution.py:363

commit v3 on v2

--- a/solution.py
+++ b/solution.py
@@ -81,13 +81,14 @@
         copy.wait()
 
 
-def pack_kernel(lateral_any, vertical_any, weight_any, out, obs_lateral, obs_vertical, obs_weight, sems):
+def pack_kernel(lateral_any, vertical_any, weight_any, out_any, out, obs_lateral, obs_vertical, obs_weight, sems, out_sems):
     copies = fetched(
         [(lateral_any, obs_lateral), (vertical_any, obs_vertical), (weight_any, obs_weight)], sems
     )
     for copy in copies:
         copy.wait()
     moments, cols, slots = obs_lateral.shape
+    copies = []
     levels = obs_vertical.shape[1]
     tiles = out.shape[0]
     cap = slots // tiles
@@ -99,6 +100,9 @@
         )
         row = jnp.concatenate([obs_weight[s : s + 1, lanes].astype(F32) for s in range(moments)], axis=1)
         out[tile, cols + levels :] = jnp.broadcast_to(row, (ROWS, row.shape[1])).astype(BF16)
+        copies += fetched([(out.at[tile], out_any.at[tile])], out_sems.at[pl.ds(tile, 1)])
+    for copy in copies:
+        copy.wait()
 
 
 def gate_kernel(data, after, out):
@@ -111,18 +115,18 @@
     for k in range((entries + 1) // 2):
         single = 2 * k + 1 >= entries
         weight = pair[k, :cols, :cols] if single else pair[k]
+        rows = []
         for s in moments:
-            rows = []
             for b in blocks:
                 part = get(s, b, 2 * k)
                 rows.append(part if single else jnp.concatenate([part, get(s, b, 2 * k + 1)], axis=1))
-            result = dot(jnp.concatenate(rows, axis=0), weight).astype(BF16)
-            for i in range(len(blocks)):
-                piece = result[i * levels : (i + 1) * levels]
-                lanes = slice(i * cols, (i + 1) * cols)
-                stage[s, 2 * k * levels : (2 * k + 1) * levels, lanes] = piece[:, :cols]
-                if not single:
-                    stage[s, (2 * k + 1) * levels : (2 * k + 2) * levels, lanes] = piece[:, cols:]
+        result = dot(jnp.concatenate(rows, axis=0), weight).astype(BF16)
+        for i, (s, n) in enumerate((s, n) for s in moments for n in range(len(blocks))):
+            piece = result[i * levels : (i + 1) * levels]
+            lanes = slice(n * cols, (n + 1) * cols)
+            stage[s, 2 * k * levels : (2 * k + 1) * levels, lanes] = piece[:, :cols]
+            if not single:
+                stage[s, (2 * k + 1) * levels : (2 * k + 2) * levels, lanes] = piece[:, cols:]
     return [(s, dot(vert[...], stage[s])) for s in moments]
 
 
@@ -282,7 +286,7 @@
 def observe_kernel(packed, incr, arrived, target, inner_base, *rest):
     moments, levels, cols_all = incr.shape
     outer_base = rest[:moments]
-    adjoint_any, image, adjoint, masked, sems = rest[moments:]
+    adjoint_any, image_any, adjoint, image, sems = rest[moments:]
     slots = target.shape[1]
     width = outer_base[0].shape[1] // 2
     cols = width // REACH
@@ -299,13 +303,18 @@
             whole = arrived[s]
         lateral = whole[:cols]
         vertical = whole[cols : cols + levels].astype(F32)
-        weight = whole[cols + levels : cols + levels + ROWS].astype(F32)[:1]
-        for b in range(blocks):
-            hit = jnp.where(block == b, 1.0, 0.0)
-            masked[s % 2, b * cols : (b + 1) * cols] = lateral * jnp.broadcast_to(hit, lateral.shape).astype(BF16)
-        along = dot(incr[s], masked[s % 2])
+        weight = whole[cols + levels :].astype(F32)[:1]
+        hits = [jnp.where(block == b, 1.0, 0.0) for b in range(blocks)]
+        fields = jnp.concatenate([incr[s, :, b * cols : (b + 1) * cols] for b in range(blocks)], axis=0)
+        seen = dot(fields, lateral)
+        along = sum(hits[b] * seen[b * levels : (b + 1) * levels] for b in range(blocks))
         image[s : s + 1] = jnp.sum(vertical * along, axis=0, keepdims=True)
-        push = dot_nt((vertical * weight).astype(BF16), masked[s % 2])
+        if s == moments - 1:
+            copies += fetched([(image, image_any)], sems.at[pl.ds(moments, 1)])
+        scaled = (vertical * weight).astype(BF16)
+        parts = [scaled * jnp.broadcast_to(hit, scaled.shape).astype(BF16) for hit in hits]
+        stacked = dot_nt(jnp.concatenate(parts, axis=0), lateral)
+        push = jnp.concatenate([stacked[b * levels : (b + 1) * levels] for b in range(blocks)], axis=1)
         adjoint[s, :, :width] = (outer_base[s][:, :width] + push[:, :width]).astype(BF16)
         adjoint[s, :, inner_lanes] = (inner_base[s] + push[:, inner_lanes]).astype(BF16)
         adjoint[s, :, cols_all - width :] = (outer_base[s][:, width:] + push[:, cols_all - width :]).astype(BF16)
@@ -339,7 +348,10 @@
             shape((tiles, height, moments * cap), BF16),
             (obs_lateral, obs_vertical, obs_weight),
             [ANY] * 3,
-            scratch=[pltpu.VMEM(a.shape, BF16) for a in (obs_lateral, obs_vertical, obs_weight)] + [semaphores((3,))],
+            out_specs=HBM,
+            scratch=[pltpu.VMEM((tiles, height, moments * cap), BF16)]
+            + [pltpu.VMEM(a.shape, BF16) for a in (obs_lateral, obs_vertical, obs_weight)]
+            + [semaphores((3,)), semaphores((tiles,))],
             cost=1,
         )
     else:
@@ -395,8 +407,8 @@
         [shape(incr.shape, BF16), shape((moments, slots), F32)],
         (incr, arrived, target, inner_base, *outer_base),
         [VMEM] * (4 + moments),
-        out_specs=[HBM, VMEM],
-        scratch=[pltpu.VMEM(incr.shape, BF16), pltpu.VMEM((2, cols_all, slots), BF16), semaphores((moments,))],
+        out_specs=[HBM, HBM],
+        scratch=[pltpu.VMEM(incr.shape, BF16), pltpu.VMEM((moments, slots), F32), semaphores((moments + 1,))],
         cost=3,
     )
     return residual, adjoint, image

time: 29.8 us -> 28.8 us (0.966)
  Pallas kernels: 13.6 us -> 12.5 us
    pallas_call x6, Pallas kernels: 13.6 us -> 12.5 us  [call(): pl.pallas_call(kernel, out_shape=out_shape, in_specs=specs, out_specs=out...]
where the time goes in v3:
time: 28.8 us; the launch traced here: 28.6 us
  Pallas kernels  12.5 us (43%)
  starting transfers between devices  11.5 us (40%)
  waiting for transfers between devices  2.65 us (9%)
  other arithmetic  1.03 us (4%)
  between operations  0.84 us (3%)
    pallas_call x6, Pallas kernels, call(): pl.pallas_call(kernel, out_shape=out_shape, in_specs=specs, out_specs=out...  12.5 us
    all_to_all x1, starting transfers between devices, on_device(): lax.all_to_all(outgoing, 'space', split_axis=0, concat_axis=0, tiled=True)  7.72 us
    ppermute x2, starting transfers between devices, exchanged(): return lax.ppermute(array, 'space', both)  3.25 us
    all_to_all x1, waiting for transfers between devices, on_device(): lax.all_to_all(outgoing, 'space', split_axis=0, concat_axis=0, tiled=True)  2.64 us
    select_n x1, other arithmetic, on_device(): jnp.where(tm == 0, incr[-1], costate[0])  1.03 us
  transfers between devices with their start and end apart: 4, of which 1 were waited for; matrix products, arithmetic and copies ran while one was open for 0% of the time, Pallas kernels for 37%

profile of v3, /device:TPU:0, one launch (start us, length us, event | category | flops | bytes accessed | tf_op | source)
XLA Modules:
  0.0 28.6 jit_solution(9030345196763105467)
XLA Ops:
  0.6 0.0 copy-start.3
  0.6 0.0 copy-start.5
  0.7 0.0 copy-start.8
  0.7 1.0 %select_bitcast_fusion = bf16[64,1024]{1,0:T(8,128)(2,1)S(1)} fusion(bf16[4,64,1024]{2,1,0:T(8,128)(2,1)} %costate.5, bf16[4,64,1024]{2,1,0:T(8,128)(2,1)} %incr.7, pred[]{:T(512)S(6)} %eq.3), kind=kLoop, calls=%fused_computation | loop fusion | flops 65536 | bytes 393217 | tf_op jit(solution)/shard_map/jit(_where)/select_n | solution.py:341
  1.7 0.0 copy-start
  1.7 0.0 copy-start.1
  1.7 0.0 copy-start.7
  1.7 0.5 %collective-permute-start = (bf16[64,1024]{1,0:T(8,128)(2,1)S(1)}, bf16[64,1024]{1,0:T(8,128)(2,1)S(1)}, u32[]{:S(2)}, u32[]{:S(2)}) collective-permute-start(bf16[64,1024]{1,0:T(8,128)(2,1)S(1)} %select_bitcast_fusion), channel_id=1, source_target_pairs={{0,1},{1,0},{2,3},{3,2},{4,5},{5,4},{6,7},{7,6},{8,9},{9,8},{10,11... | collective-permute-start | bytes 393224 | tf_op jit(solution)/shard_map/ppermute | solution.py:341
  2.3 0.0 copy-done.3
  2.3 0.0 copy-done.5
  2.3 0.0 copy-done.8
  2.3 1.3 %shard_map.124.data = bf16[8,200,128]{2,1,0:T(8,128)(2,1)} custom-call(bf16[4,128,256]{2,1,0:T(8,128)(2,1)S(1)} %copy-done.3, bf16[4,64,256]{2,1,0:T(8,128)(2,1)S(1)} %copy-done.5, bf16[4,256]{1,0:T(4,128)(2,1)S(1)} %copy-done.8), custom_call_target="tpu_custom_call" | custom-call | flops 1000000000 | bytes 1000000 | tf_op jit(solution)/shard_map/pallas_call | solution.py:36
  3.6 0.0 collective-permute-done.crossed
  3.6 0.0 copy-done
  3.6 0.0 copy-done.1
  3.6 0.0 copy-done.7
  3.6 0.3 shard_map.121
  3.9 2.6 %collective-permute-start.1 = (bf16[456,256]{1,0:T(8,128)(2,1)S(1)}, bf16[456,256]{1,0:T(8,128)(2,1)S(1)}, u32[]{:S(2)}, u32[]{:S(2)}) collective-permute-start(bf16[456,256]{1,0:T(8,128)(2,1)S(1)} %get-tuple-element.19.after), channel_id=1, source_target_pairs={{0,2},{4,6},{8,10},{12,14},{2,0},{6,4},{10,8},{14,12},{1,3},{5,7},... | collective-permute-start | bytes 700424 | tf_op jit(solution)/shard_map/ppermute | solution.py:31
  6.5 0.7 %collective-permute-start.2 = (bf16[456,256]{1,0:T(8,128)(2,1)S(1)}, bf16[456,256]{1,0:T(8,128)(2,1)S(1)}, u32[]{:S(2)}, u32[]{:S(2)}) collective-permute-start(bf16[456,256]{1,0:T(8,128)(2,1)S(1)} %get-tuple-element.20), channel_id=1, source_target_pairs={{2,4},{6,8},{10,12},{4,2},{8,6},{12,10},{3,5},{7,9},{11,13},{5,3},... | collective-permute-start | bytes 700424 | tf_op jit(solution)/shard_map/ppermute | solution.py:31
  7.2 0.0 copy-start.2
  7.2 0.0 copy-start.4
  7.2 0.0 copy-start.6
  7.2 0.0 copy-start.9
  7.2 7.7 %all-to-all-start = ((bf16[8,200,128]{2,1,0:T(8,128)(2,1)}), bf16[8,200,128]{2,1,0:T(8,128)(2,1)S(1)}, u32[]{:S(2)}, u32[]{:S(2)}) async-start(bf16[8,200,128]{2,1,0:T(8,128)(2,1)} %shard_map.125), calls=%async_computation | async-start | bytes 819200 | tf_op jit(solution)/shard_map/all_to_all | solution.py:375
  14.9 0.0 copy-done.2
  14.9 0.0 copy-done.4
  15.0 0.0 copy-done.6
  15.0 0.0 copy-done.9
  15.0 4.4 %shard_map.122 = (bf16[4,64,512]{2,1,0:T(8,128)(2,1)S(1)}, f32[4,64,512]{2,1,0:T(8,128)S(1)}, bf16[5,256,256]{2,1,0:T(8,128)(2,1)S(1)}, bf16[5,256,256]{2,1,0:T(...) custom-call(s32[8,9]{1,0:T(8,128)S(1)} %copy-done.7, ...), custom_call_target="tpu_custom_call" | custom-call | flops 4000000000 | bytes 4000000 | tf_op jit(solution)/shard_map/pallas_call | solution.py:36
  19.4 0.0 collective-permute-done.1.first
  19.4 0.0 collective-permute-done.2.second
  19.4 5.0 %shard_map.123 = (bf16[4,64,1024]{2,1,0:T(8,128)(2,1)}, f32[64,512]{1,0:T(8,128)S(1)}, f32[64,512]{1,0:T(8,128)S(1)}, f32[64,512]{1,0:T(8,128)S(1)}, f32[64,512]{1,0:T(8,128)S(1)}) custom-call(s32[8,9]{1,0:T(8,128)S(1)} %copy-done.7, bf16[4,64,1024]{2,1,0:T(8,128)(2,1)S(1)} %copy-done.1, bf16[4,64,1024]{2,1,0:T(8,128)(2,1)S(1)} %copy-done, ...), custom_call_target="tpu_custom_call" | custom-call | flops 4000000000 | bytes 4000000 | tf_op jit(solution)/shard_map/pallas_call | solution.py:36
  24.4 2.6 %all-to-all-done.arrived = bf16[8,200,128]{2,1,0:T(8,128)(2,1)S(1)} async-done(((bf16[8,200,128]{2,1,0:T(8,128)(2,1)}), bf16[8,200,128]{2,1,0:T(8,128)(2,1)S(1)}, u32[]{:S(2)}, u32[]{:S(2)}) %all-to-all-start) | async-done | bytes 409632 | tf_op jit(solution)/shard_map/all_to_all | solution.py:375
  27.0 1.5 %shard_map.126 = (bf16[4,64,1024]{2,1,0:T(8,128)(2,1)}, f32[4,256]{1,0:T(4,128)}) custom-call(bf16[4,64,1024]{2,1,0:T(8,128)(2,1)S(1)} %copy-done.1, bf16[8,200,128]{2,1,0:T(8,128)(2,1)S(1)} %all-to-all-done.arrived, s32[4,256]{1,0:T(4,128)S(1)} %get-tuple-element.27.target, f32[4,64,512]{2,1,0:T(8,128)S(1)} %get-tuple-element.28.inner_base, ...), custom_call_target="tpu_custom_call" | custom-call | flops 3000000000 | bytes 3000000 | tf_op jit(solution)/shard_map/pallas_call | solution.py:36
  (1 shorter events, 0.0 us)
Async XLA Ops:
  0.6 1.6 %copy-start.3 = (bf16[4,128,256]{2,1,0:T(8,128)(2,1)S(1)}, bf16[4,128,256]{2,1,0:T(8,128)(2,1)}, u32[]{:S(2)}) copy-start(bf16[4,128,256]{2,1,0:T(8,128)(2,1)} %lateral_any.1) | copy-start | bytes 786436
  0.6 1.6 %copy-start.5 = (bf16[4,64,256]{2,1,0:T(8,128)(2,1)S(1)}, bf16[4,64,256]{2,1,0:T(8,128)(2,1)}, u32[]{:S(2)}) copy-start(bf16[4,64,256]{2,1,0:T(8,128)(2,1)} %vertical_any.1) | copy-start | bytes 393220
  0.7 1.6 %copy-start.8 = (bf16[4,256]{1,0:T(4,128)(2,1)S(1)}, bf16[4,256]{1,0:T(4,128)(2,1)}, u32[]{:S(2)}) copy-start(bf16[4,256]{1,0:T(4,128)(2,1)} %weight_any.1) | copy-start | bytes 6148
  1.7 1.9 %copy-start = (bf16[4,64,1024]{2,1,0:T(8,128)(2,1)S(1)}, bf16[4,64,1024]{2,1,0:T(8,128)(2,1)}, u32[]{:S(2)}) copy-start(bf16[4,64,1024]{2,1,0:T(8,128)(2,1)} %costate.5) | copy-start | bytes 1572868
  1.7 1.9 %copy-start.1 = (bf16[4,64,1024]{2,1,0:T(8,128)(2,1)S(1)}, bf16[4,64,1024]{2,1,0:T(8,128)(2,1)}, u32[]{:S(2)}) copy-start(bf16[4,64,1024]{2,1,0:T(8,128)(2,1)} %incr.7) | copy-start | bytes 1572868
  1.7 1.9 %copy-start.7 = (s32[8,9]{1,0:T(8,128)S(1)}, s32[8,9]{1,0:T(8,128)}, u32[]{:S(2)}) copy-start(s32[8,9]{1,0:T(8,128)} %near.3) | copy-start | bytes 868
  1.7 1.8 %collective-permute-start = (bf16[64,1024]{1,0:T(8,128)(2,1)S(1)}, bf16[64,1024]{1,0:T(8,128)(2,1)S(1)}, u32[]{:S(2)}, u32[]{:S(2)}) collective-permute-start(bf16[64,1024]{1,0:T(8,128)(2,1)S(1)} %select_bitcast_fusion), channel_id=1, source_target_pairs={{0,1},{1,0},{2,3},{3,2},{4,5},{5,4},{6,7},{7,6},{8,9},{9,8},{10,11... | collective-permute-start | bytes 393224 | tf_op jit(solution)/shard_map/ppermute | solution.py:341
  3.9 15.5 %collective-permute-start.1 = (bf16[456,256]{1,0:T(8,128)(2,1)S(1)}, bf16[456,256]{1,0:T(8,128)(2,1)S(1)}, u32[]{:S(2)}, u32[]{:S(2)}) collective-permute-start(bf16[456,256]{1,0:T(8,128)(2,1)S(1)} %get-tuple-element.19.after), channel_id=1, source_target_pairs={{0,2},{4,6},{8,10},{12,14},{2,0},{6,4},{10,8},{14,12},{1,3},{5,7},... | collective-permute-start | bytes 700424 | tf_op jit(solution)/shard_map/ppermute | solution.py:31
  6.5 12.9 %collective-permute-start.2 = (bf16[456,256]{1,0:T(8,128)(2,1)S(1)}, bf16[456,256]{1,0:T(8,128)(2,1)S(1)}, u32[]{:S(2)}, u32[]{:S(2)}) collective-permute-start(bf16[456,256]{1,0:T(8,128)(2,1)S(1)} %get-tuple-element.20), channel_id=1, source_target_pairs={{2,4},{6,8},{10,12},{4,2},{8,6},{12,10},{3,5},{7,9},{11,13},{5,3},... | collective-permute-start | bytes 700424 | tf_op jit(solution)/shard_map/ppermute | solution.py:31
  7.2 7.8 %copy-start.2 = (bf16[9,128,128]{2,1,0:T(8,128)(2,1)S(1)}, bf16[9,128,128]{2,1,0:T(8,128)(2,1)}, u32[]{:S(2)}) copy-start(bf16[9,128,128]{2,1,0:T(8,128)(2,1)} %lateral_mix.1) | copy-start | bytes 884740
  7.2 7.8 %copy-start.4 = (bf16[9,64,64]{2,1,0:T(8,128)(2,1)S(1)}, bf16[9,64,64]{2,1,0:T(8,128)(2,1)}, u32[]{:S(2)}) copy-start(bf16[9,64,64]{2,1,0:T(8,128)(2,1)} %vertical_mix.1) | copy-start | bytes 221188
  7.2 7.8 %copy-start.6 = (s32[4,256]{1,0:T(4,128)S(1)}, s32[4,256]{1,0:T(4,128)}, u32[]{:S(2)}) copy-start(s32[4,256]{1,0:T(4,128)} %owner.1) | copy-start | bytes 12292
  7.2 7.8 %copy-start.9 = (s32[4,8]{1,0:T(4,128)S(1)}, s32[4,8]{1,0:T(4,128)}, u32[]{:S(2)}) copy-start(s32[4,8]{1,0:T(4,128)} %counts.1) | copy-start | bytes 388
  7.2 19.8 %all-to-all-start = ((bf16[8,200,128]{2,1,0:T(8,128)(2,1)}), bf16[8,200,128]{2,1,0:T(8,128)(2,1)S(1)}, u32[]{:S(2)}, u32[]{:S(2)}) async-start(bf16[8,200,128]{2,1,0:T(8,128)(2,1)} %shard_map.125), calls=%async_computation | async-start | bytes 819200 | tf_op jit(solution)/shard_map/all_to_all | solution.py:375

commit v4 on v3

--- a/solution.py
+++ b/solution.py
@@ -81,12 +81,7 @@
         copy.wait()
 
 
-def pack_kernel(lateral_any, vertical_any, weight_any, out_any, out, obs_lateral, obs_vertical, obs_weight, sems, out_sems):
-    copies = fetched(
-        [(lateral_any, obs_lateral), (vertical_any, obs_vertical), (weight_any, obs_weight)], sems
-    )
-    for copy in copies:
-        copy.wait()
+def pack_kernel(obs_lateral, obs_vertical, obs_weight, out_any, out, out_sems):
     moments, cols, slots = obs_lateral.shape
     copies = []
     levels = obs_vertical.shape[1]
@@ -170,9 +165,9 @@
         for b in range(n - REACH, n + REACH + 1):
             at = slice(b * cols, (b + 1) * cols)
             source = crossed[:, at] if s == moments - 1 else costate[s + 1, :, at]
-            term = jnp.where(near[b, j] == anchor + n, source, jnp.zeros_like(source))
+            term = jnp.where(near[b, j] == anchor + n, source, jnp.zeros_like(source)).astype(F32)
             total = term if total is None else total + term
-        return total
+        return total.astype(BF16)
 
     def run_forward(which):
         for s, pushed in mixed(forward, which, inner, entries, pair_fwd, vert_fwd, stage):
@@ -246,8 +241,8 @@
                 offset = (left if b < 0 else right)[row : row + 1, j : j + 1]
                 hit = jnp.where(offset == float(n - b), 1.0, 0.0)
                 term = source * jnp.broadcast_to(hit, source.shape).astype(BF16)
-            total = term if total is None else total + term
-        return total
+            total = term.astype(F32) if total is None else total + term.astype(F32)
+        return total.astype(BF16)
 
     def ends(field, s):
         return jnp.concatenate([field[s, :, :width], field[s, :, cols_all - width :]], axis=1).astype(F32)
@@ -347,11 +342,9 @@
             pack_kernel,
             shape((tiles, height, moments * cap), BF16),
             (obs_lateral, obs_vertical, obs_weight),
-            [ANY] * 3,
+            [VMEM] * 3,
             out_specs=HBM,
-            scratch=[pltpu.VMEM((tiles, height, moments * cap), BF16)]
-            + [pltpu.VMEM(a.shape, BF16) for a in (obs_lateral, obs_vertical, obs_weight)]
-            + [semaphores((3,)), semaphores((tiles,))],
+            scratch=[pltpu.VMEM((tiles, height, moments * cap), BF16), semaphores((tiles,))],
             cost=1,
         )
     else:

time: 28.8 us -> 28.6 us (level)
  waiting for transfers between devices: 2.65 us -> 1.2 us
  Pallas kernels: 12.5 us -> 13.6 us
    all_to_all x1, waiting for transfers between devices: 2.64 us -> 1.19 us  [on_device(): lax.all_to_all(outgoing, 'space', split_axis=0, concat_axis=0, tiled=True)]
    pallas_call x6, Pallas kernels: 12.5 us -> 13.6 us  [call(): pl.pallas_call(kernel, out_shape=out_shape, in_specs=specs, out_specs=out...]
  transfers between devices with their start and end apart: 4 -> 4, of which waited for: 1 -> 1; matrix products, arithmetic and copies ran while one was open for 0% -> 0% of each run, Pallas kernels for 37% -> 42%
where the time goes in v4:
time: 28.6 us; the launch traced here: 28.4 us
  Pallas kernels  13.6 us (48%)
  starting transfers between devices  11.7 us (41%)
  waiting for transfers between devices  1.2 us (4%)
  other arithmetic  1.03 us (4%)
  between operations  0.84 us (3%)
    pallas_call x6, Pallas kernels, call(): pl.pallas_call(kernel, out_shape=out_shape, in_specs=specs, out_specs=out...  13.6 us
    all_to_all x1, starting transfers between devices, on_device(): lax.all_to_all(outgoing, 'space', split_axis=0, concat_axis=0, tiled=True)  7.72 us
    ppermute x2, starting transfers between devices, exchanged(): return lax.ppermute(array, 'space', both)  3.43 us
    all_to_all x1, waiting for transfers between devices, on_device(): lax.all_to_all(outgoing, 'space', split_axis=0, concat_axis=0, tiled=True)  1.19 us
    select_n x1, other arithmetic, on_device(): jnp.where(tm == 0, incr[-1], costate[0])  1.03 us
  transfers between devices with their start and end apart: 4, of which 1 were waited for; matrix products, arithmetic and copies ran while one was open for 0% of the time, Pallas kernels for 42%

profile of v4, /device:TPU:0, one launch (start us, length us, event | category | flops | bytes accessed | tf_op | source)
XLA Modules:
  0.0 28.4 jit_solution(16587473319188099052)
XLA Ops:
  0.6 0.0 copy-start.3
  0.6 0.0 copy-start.5
  0.7 0.0 copy-start.8
  0.7 1.0 %select_bitcast_fusion = bf16[64,1024]{1,0:T(8,128)(2,1)S(1)} fusion(bf16[4,64,1024]{2,1,0:T(8,128)(2,1)} %costate.5, bf16[4,64,1024]{2,1,0:T(8,128)(2,1)} %incr.7, pred[]{:T(512)S(6)} %eq.3), kind=kLoop, calls=%fused_computation | loop fusion | flops 65536 | bytes 393217 | tf_op jit(solution)/shard_map/jit(_where)/select_n | solution.py:336
  1.7 0.0 copy-start
  1.7 0.0 copy-start.1
  1.7 0.0 copy-start.7
  1.7 0.5 %collective-permute-start = (bf16[64,1024]{1,0:T(8,128)(2,1)S(1)}, bf16[64,1024]{1,0:T(8,128)(2,1)S(1)}, u32[]{:S(2)}, u32[]{:S(2)}) collective-permute-start(bf16[64,1024]{1,0:T(8,128)(2,1)S(1)} %select_bitcast_fusion), channel_id=1, source_target_pairs={{0,1},{1,0},{2,3},{3,2},{4,5},{5,4},{6,7},{7,6},{8,9},{9,8},{10,11... | collective-permute-start | bytes 393224 | tf_op jit(solution)/shard_map/ppermute | solution.py:336
  2.3 0.0 copy-done.3
  2.3 0.0 copy-done.5
  2.3 0.0 copy-done.8
  2.3 1.1 %shard_map.124.data = bf16[8,200,128]{2,1,0:T(8,128)(2,1)} custom-call(bf16[4,128,256]{2,1,0:T(8,128)(2,1)S(1)} %copy-done.3, bf16[4,64,256]{2,1,0:T(8,128)(2,1)S(1)} %copy-done.5, bf16[4,256]{1,0:T(4,128)(2,1)S(1)} %copy-done.8), custom_call_target="tpu_custom_call" | custom-call | flops 1000000000 | bytes 1000000 | tf_op jit(solution)/shard_map/pallas_call | solution.py:36
  3.4 0.0 collective-permute-done.crossed
  3.4 0.0 copy-done
  3.4 0.0 copy-done.1
  3.4 0.0 copy-done.7
  3.4 0.3 shard_map.121
  3.7 2.8 %collective-permute-start.1 = (bf16[456,256]{1,0:T(8,128)(2,1)S(1)}, bf16[456,256]{1,0:T(8,128)(2,1)S(1)}, u32[]{:S(2)}, u32[]{:S(2)}) collective-permute-start(bf16[456,256]{1,0:T(8,128)(2,1)S(1)} %get-tuple-element.19.after), channel_id=1, source_target_pairs={{0,2},{4,6},{8,10},{12,14},{2,0},{6,4},{10,8},{14,12},{1,3},{5,7},... | collective-permute-start | bytes 700424 | tf_op jit(solution)/shard_map/ppermute | solution.py:31
  6.4 0.7 %collective-permute-start.2 = (bf16[456,256]{1,0:T(8,128)(2,1)S(1)}, bf16[456,256]{1,0:T(8,128)(2,1)S(1)}, u32[]{:S(2)}, u32[]{:S(2)}) collective-permute-start(bf16[456,256]{1,0:T(8,128)(2,1)S(1)} %get-tuple-element.20), channel_id=1, source_target_pairs={{2,4},{6,8},{10,12},{4,2},{8,6},{12,10},{3,5},{7,9},{11,13},{5,3},... | collective-permute-start | bytes 700424 | tf_op jit(solution)/shard_map/ppermute | solution.py:31
  7.1 0.0 copy-start.2
  7.1 0.0 copy-start.4
  7.2 0.0 copy-start.6
  7.2 0.0 copy-start.9
  7.2 7.7 %all-to-all-start = ((bf16[8,200,128]{2,1,0:T(8,128)(2,1)}), bf16[8,200,128]{2,1,0:T(8,128)(2,1)S(1)}, u32[]{:S(2)}, u32[]{:S(2)}) async-start(bf16[8,200,128]{2,1,0:T(8,128)(2,1)} %shard_map.125), calls=%async_computation | async-start | bytes 819200 | tf_op jit(solution)/shard_map/all_to_all | solution.py:368
  14.9 0.0 copy-done.2
  14.9 0.0 copy-done.4
  14.9 0.0 copy-done.6
  14.9 0.0 copy-done.9
  14.9 5.1 %shard_map.122 = (bf16[4,64,512]{2,1,0:T(8,128)(2,1)S(1)}, f32[4,64,512]{2,1,0:T(8,128)S(1)}, bf16[5,256,256]{2,1,0:T(8,128)(2,1)S(1)}, bf16[5,256,256]{2,1,0:T(...) custom-call(s32[8,9]{1,0:T(8,128)S(1)} %copy-done.7, ...), custom_call_target="tpu_custom_call" | custom-call | flops 4000000000 | bytes 4000000 | tf_op jit(solution)/shard_map/pallas_call | solution.py:36
  20.0 0.0 collective-permute-done.1.first
  20.1 0.0 collective-permute-done.2.second
  20.1 5.6 %shard_map.123 = (bf16[4,64,1024]{2,1,0:T(8,128)(2,1)}, f32[64,512]{1,0:T(8,128)S(1)}, f32[64,512]{1,0:T(8,128)S(1)}, f32[64,512]{1,0:T(8,128)S(1)}, f32[64,512]{1,0:T(8,128)S(1)}) custom-call(s32[8,9]{1,0:T(8,128)S(1)} %copy-done.7, bf16[4,64,1024]{2,1,0:T(8,128)(2,1)S(1)} %copy-done.1, bf16[4,64,1024]{2,1,0:T(8,128)(2,1)S(1)} %copy-done, ...), custom_call_target="tpu_custom_call" | custom-call | flops 4000000000 | bytes 4000000 | tf_op jit(solution)/shard_map/pallas_call | solution.py:36
  25.7 1.2 %all-to-all-done.arrived = bf16[8,200,128]{2,1,0:T(8,128)(2,1)S(1)} async-done(((bf16[8,200,128]{2,1,0:T(8,128)(2,1)}), bf16[8,200,128]{2,1,0:T(8,128)(2,1)S(1)}, u32[]{:S(2)}, u32[]{:S(2)}) %all-to-all-start) | async-done | bytes 409632 | tf_op jit(solution)/shard_map/all_to_all | solution.py:368
  26.9 1.5 %shard_map.126 = (bf16[4,64,1024]{2,1,0:T(8,128)(2,1)}, f32[4,256]{1,0:T(4,128)}) custom-call(bf16[4,64,1024]{2,1,0:T(8,128)(2,1)S(1)} %copy-done.1, bf16[8,200,128]{2,1,0:T(8,128)(2,1)S(1)} %all-to-all-done.arrived, s32[4,256]{1,0:T(4,128)S(1)} %get-tuple-element.27.target, f32[4,64,512]{2,1,0:T(8,128)S(1)} %get-tuple-element.28.inner_base, ...), custom_call_target="tpu_custom_call" | custom-call | flops 3000000000 | bytes 3000000 | tf_op jit(solution)/shard_map/pallas_call | solution.py:36
  (1 shorter events, 0.0 us)
Async XLA Ops:
  0.6 1.6 %copy-start.3 = (bf16[4,128,256]{2,1,0:T(8,128)(2,1)S(1)}, bf16[4,128,256]{2,1,0:T(8,128)(2,1)}, u32[]{:S(2)}) copy-start(bf16[4,128,256]{2,1,0:T(8,128)(2,1)} %obs_lateral.1) | copy-start | bytes 786436
  0.6 1.6 %copy-start.5 = (bf16[4,64,256]{2,1,0:T(8,128)(2,1)S(1)}, bf16[4,64,256]{2,1,0:T(8,128)(2,1)}, u32[]{:S(2)}) copy-start(bf16[4,64,256]{2,1,0:T(8,128)(2,1)} %obs_vertical.1) | copy-start | bytes 393220
  0.7 1.6 %copy-start.8 = (bf16[4,256]{1,0:T(4,128)(2,1)S(1)}, bf16[4,256]{1,0:T(4,128)(2,1)}, u32[]{:S(2)}) copy-start(bf16[4,256]{1,0:T(4,128)(2,1)} %obs_weight.1) | copy-start | bytes 6148
  1.7 1.7 %copy-start = (bf16[4,64,1024]{2,1,0:T(8,128)(2,1)S(1)}, bf16[4,64,1024]{2,1,0:T(8,128)(2,1)}, u32[]{:S(2)}) copy-start(bf16[4,64,1024]{2,1,0:T(8,128)(2,1)} %costate.5) | copy-start | bytes 1572868
  1.7 1.7 %copy-start.1 = (bf16[4,64,1024]{2,1,0:T(8,128)(2,1)S(1)}, bf16[4,64,1024]{2,1,0:T(8,128)(2,1)}, u32[]{:S(2)}) copy-start(bf16[4,64,1024]{2,1,0:T(8,128)(2,1)} %incr.7) | copy-start | bytes 1572868
  1.7 1.7 %copy-start.7 = (s32[8,9]{1,0:T(8,128)S(1)}, s32[8,9]{1,0:T(8,128)}, u32[]{:S(2)}) copy-start(s32[8,9]{1,0:T(8,128)} %near.3) | copy-start | bytes 868
  1.7 1.6 %collective-permute-start = (bf16[64,1024]{1,0:T(8,128)(2,1)S(1)}, bf16[64,1024]{1,0:T(8,128)(2,1)S(1)}, u32[]{:S(2)}, u32[]{:S(2)}) collective-permute-start(bf16[64,1024]{1,0:T(8,128)(2,1)S(1)} %select_bitcast_fusion), channel_id=1, source_target_pairs={{0,1},{1,0},{2,3},{3,2},{4,5},{5,4},{6,7},{7,6},{8,9},{9,8},{10,11... | collective-permute-start | bytes 393224 | tf_op jit(solution)/shard_map/ppermute | solution.py:336
  3.7 16.4 %collective-permute-start.1 = (bf16[456,256]{1,0:T(8,128)(2,1)S(1)}, bf16[456,256]{1,0:T(8,128)(2,1)S(1)}, u32[]{:S(2)}, u32[]{:S(2)}) collective-permute-start(bf16[456,256]{1,0:T(8,128)(2,1)S(1)} %get-tuple-element.19.after), channel_id=1, source_target_pairs={{0,2},{4,6},{8,10},{12,14},{2,0},{6,4},{10,8},{14,12},{1,3},{5,7},... | collective-permute-start | bytes 700424 | tf_op jit(solution)/shard_map/ppermute | solution.py:31
  6.4 13.6 %collective-permute-start.2 = (bf16[456,256]{1,0:T(8,128)(2,1)S(1)}, bf16[456,256]{1,0:T(8,128)(2,1)S(1)}, u32[]{:S(2)}, u32[]{:S(2)}) collective-permute-start(bf16[456,256]{1,0:T(8,128)(2,1)S(1)} %get-tuple-element.20), channel_id=1, source_target_pairs={{2,4},{6,8},{10,12},{4,2},{8,6},{12,10},{3,5},{7,9},{11,13},{5,3},... | collective-permute-start | bytes 700424 | tf_op jit(solution)/shard_map/ppermute | solution.py:31
  7.1 7.8 %copy-start.2 = (bf16[9,128,128]{2,1,0:T(8,128)(2,1)S(1)}, bf16[9,128,128]{2,1,0:T(8,128)(2,1)}, u32[]{:S(2)}) copy-start(bf16[9,128,128]{2,1,0:T(8,128)(2,1)} %lateral_mix.1) | copy-start | bytes 884740
  7.1 7.8 %copy-start.4 = (bf16[9,64,64]{2,1,0:T(8,128)(2,1)S(1)}, bf16[9,64,64]{2,1,0:T(8,128)(2,1)}, u32[]{:S(2)}) copy-start(bf16[9,64,64]{2,1,0:T(8,128)(2,1)} %vertical_mix.1) | copy-start | bytes 221188
  7.2 7.8 %copy-start.6 = (s32[4,256]{1,0:T(4,128)S(1)}, s32[4,256]{1,0:T(4,128)}, u32[]{:S(2)}) copy-start(s32[4,256]{1,0:T(4,128)} %owner.1) | copy-start | bytes 12292
  7.2 7.8 %copy-start.9 = (s32[4,8]{1,0:T(4,128)S(1)}, s32[4,8]{1,0:T(4,128)}, u32[]{:S(2)}) copy-start(s32[4,8]{1,0:T(4,128)} %counts.1) | copy-start | bytes 388
  7.2 19.7 %all-to-all-start = ((bf16[8,200,128]{2,1,0:T(8,128)(2,1)}), bf16[8,200,128]{2,1,0:T(8,128)(2,1)S(1)}, u32[]{:S(2)}, u32[]{:S(2)}) async-start(bf16[8,200,128]{2,1,0:T(8,128)(2,1)} %shard_map.125), calls=%async_computation | async-start | bytes 819200 | tf_op jit(solution)/shard_map/all_to_all | solution.py:368

commit v5 on v4

--- a/solution.py
+++ b/solution.py
@@ -8,8 +8,7 @@
 from jax.sharding import PartitionSpec as P
 
 REACH = 2
-ROWS = 8
-FULL = 63.6
+ROWS = 16
 BF16 = jnp.bfloat16
 F32 = jnp.float32
 VMEM = pl.BlockSpec(memory_space=pltpu.VMEM)
@@ -40,7 +39,7 @@
         out_specs=out_specs or ([VMEM] * len(out_shape) if multiple else VMEM),
         scratch_shapes=list(scratch),
         input_output_aliases=aliases or {},
-        compiler_params=pltpu.CompilerParams(vmem_limit_bytes=int(limit * 1024 * 1024)),
+        compiler_params=pltpu.CompilerParams(vmem_limit_bytes=limit * 1024 * 1024),
         cost_estimate=pl.CostEstimate(flops=cost * 1_000_000_000, bytes_accessed=cost * 1_000_000, transcendentals=0),
     )(*args)
 
@@ -73,7 +72,7 @@
     fetch.wait()
     own = lax.broadcasted_iota(jnp.int32, near.shape, 0) + place * blocks
     distance = (near[...] - own).astype(F32)
-    distance = distance.astype(BF16)
+    distance = jnp.concatenate([distance, jnp.zeros((ROWS - blocks, entries), F32)], axis=0).astype(BF16)
     for target in (first, second):
         target[len(slabs) * levels :] = jnp.zeros((ROWS, width), BF16)
         target[len(slabs) * levels :, :entries] = distance

time: 28.6 us -> 29 us (1.014)
  waiting for transfers between devices: 1.2 us -> 1.56 us
    all_to_all x1, waiting for transfers between devices: 1.19 us -> 1.55 us  [on_device(): lax.all_to_all(outgoing, 'space', split_axis=0, concat_axis=0, tiled=True)]
  transfers between devices with their start and end apart: 4 -> 4, of which waited for: 1 -> 1; matrix products, arithmetic and copies ran while one was open for 0% -> 0% of each run, Pallas kernels for 42% -> 41%
where the time goes in v5:
time: 29 us; the launch traced here: 28.7 us
  Pallas kernels  13.6 us (47%)
  starting transfers between devices  11.7 us (40%)
  waiting for transfers between devices  1.56 us (5%)
  other arithmetic  1.03 us (4%)
  between operations  0.84 us (3%)
    pallas_call x6, Pallas kernels, call(): pl.pallas_call(kernel, out_shape=out_shape, in_specs=specs, out_specs=out...  13.6 us
    all_to_all x1, starting transfers between devices, on_device(): lax.all_to_all(outgoing, 'space', split_axis=0, concat_axis=0, tiled=True)  7.72 us
    ppermute x2, starting transfers between devices, exchanged(): return lax.ppermute(array, 'space', both)  3.43 us
    all_to_all x1, waiting for transfers between devices, on_device(): lax.all_to_all(outgoing, 'space', split_axis=0, concat_axis=0, tiled=True)  1.55 us
    select_n x1, other arithmetic, on_device(): jnp.where(tm == 0, incr[-1], costate[0])  1.03 us
  transfers between devices with their start and end apart: 4, of which 1 were waited for; matrix products, arithmetic and copies ran while one was open for 0% of the time, Pallas kernels for 41%

profile of v5, /device:TPU:0, one launch (start us, length us, event | category | flops | bytes accessed | tf_op | source)
XLA Modules:
  0.0 28.7 jit_solution(10899410826988229240)
XLA Ops:
  0.6 0.0 copy-start.3
  0.6 0.0 copy-start.5
  0.7 0.0 copy-start.8
  0.7 1.0 %select_bitcast_fusion = bf16[64,1024]{1,0:T(8,128)(2,1)S(1)} fusion(bf16[4,64,1024]{2,1,0:T(8,128)(2,1)} %costate.5, bf16[4,64,1024]{2,1,0:T(8,128)(2,1)} %incr.7, pred[]{:T(512)S(6)} %eq.3), kind=kLoop, calls=%fused_computation | loop fusion | flops 65536 | bytes 393217 | tf_op jit(solution)/shard_map/jit(_where)/select_n | solution.py:335
  1.7 0.0 copy-start
  1.7 0.0 copy-start.1
  1.7 0.0 copy-start.7
  1.7 0.5 %collective-permute-start = (bf16[64,1024]{1,0:T(8,128)(2,1)S(1)}, bf16[64,1024]{1,0:T(8,128)(2,1)S(1)}, u32[]{:S(2)}, u32[]{:S(2)}) collective-permute-start(bf16[64,1024]{1,0:T(8,128)(2,1)S(1)} %select_bitcast_fusion), channel_id=1, source_target_pairs={{0,1},{1,0},{2,3},{3,2},{4,5},{5,4},{6,7},{7,6},{8,9},{9,8},{10,11... | collective-permute-start | bytes 393224 | tf_op jit(solution)/shard_map/ppermute | solution.py:335
  2.3 0.0 copy-done.3
  2.3 0.0 copy-done.5
  2.3 0.0 copy-done.8
  2.3 1.1 %shard_map.124.data = bf16[8,208,128]{2,1,0:T(8,128)(2,1)} custom-call(bf16[4,128,256]{2,1,0:T(8,128)(2,1)S(1)} %copy-done.3, bf16[4,64,256]{2,1,0:T(8,128)(2,1)S(1)} %copy-done.5, bf16[4,256]{1,0:T(4,128)(2,1)S(1)} %copy-done.8), custom_call_target="tpu_custom_call" | custom-call | flops 1000000000 | bytes 1000000 | tf_op jit(solution)/shard_map/pallas_call | solution.py:35
  3.4 0.0 collective-permute-done.crossed
  3.4 0.0 copy-done
  3.4 0.0 copy-done.1
  3.4 0.0 copy-done.7
  3.4 0.3 shard_map.121
  3.7 2.8 %collective-permute-start.1 = (bf16[464,256]{1,0:T(8,128)(2,1)S(1)}, bf16[464,256]{1,0:T(8,128)(2,1)S(1)}, u32[]{:S(2)}, u32[]{:S(2)}) collective-permute-start(bf16[464,256]{1,0:T(8,128)(2,1)S(1)} %get-tuple-element.19.after), channel_id=1, source_target_pairs={{0,2},{4,6},{8,10},{12,14},{2,0},{6,4},{10,8},{14,12},{1,3},{5,7},... | collective-permute-start | bytes 712712 | tf_op jit(solution)/shard_map/ppermute | solution.py:30
  6.4 0.7 %collective-permute-start.2 = (bf16[464,256]{1,0:T(8,128)(2,1)S(1)}, bf16[464,256]{1,0:T(8,128)(2,1)S(1)}, u32[]{:S(2)}, u32[]{:S(2)}) collective-permute-start(bf16[464,256]{1,0:T(8,128)(2,1)S(1)} %get-tuple-element.20), channel_id=1, source_target_pairs={{2,4},{6,8},{10,12},{4,2},{8,6},{12,10},{3,5},{7,9},{11,13},{5,3},... | collective-permute-start | bytes 712712 | tf_op jit(solution)/shard_map/ppermute | solution.py:30
  7.1 0.0 copy-start.2
  7.1 0.0 copy-start.4
  7.2 0.0 copy-start.6
  7.2 0.0 copy-start.9
  7.2 7.7 %all-to-all-start = ((bf16[8,208,128]{2,1,0:T(8,128)(2,1)}), bf16[8,208,128]{2,1,0:T(8,128)(2,1)S(1)}, u32[]{:S(2)}, u32[]{:S(2)}) async-start(bf16[8,208,128]{2,1,0:T(8,128)(2,1)} %shard_map.125), calls=%async_computation | async-start | bytes 851968 | tf_op jit(solution)/shard_map/all_to_all | solution.py:367
  14.9 0.0 copy-done.2
  14.9 0.0 copy-done.4
  14.9 0.0 copy-done.6
  14.9 0.0 copy-done.9
  14.9 5.1 %shard_map.122 = (bf16[4,64,512]{2,1,0:T(8,128)(2,1)S(1)}, f32[4,64,512]{2,1,0:T(8,128)S(1)}, bf16[5,256,256]{2,1,0:T(8,128)(2,1)S(1)}, bf16[5,256,256]{2,1,0:T(...) custom-call(s32[8,9]{1,0:T(8,128)S(1)} %copy-done.7, ...), custom_call_target="tpu_custom_call" | custom-call | flops 4000000000 | bytes 4000000 | tf_op jit(solution)/shard_map/pallas_call | solution.py:35
  20.0 0.0 collective-permute-done.1.first
  20.1 0.0 collective-permute-done.2.second
  20.1 5.6 %shard_map.123 = (bf16[4,64,1024]{2,1,0:T(8,128)(2,1)}, f32[64,512]{1,0:T(8,128)S(1)}, f32[64,512]{1,0:T(8,128)S(1)}, f32[64,512]{1,0:T(8,128)S(1)}, f32[64,512]{1,0:T(8,128)S(1)}) custom-call(s32[8,9]{1,0:T(8,128)S(1)} %copy-done.7, bf16[4,64,1024]{2,1,0:T(8,128)(2,1)S(1)} %copy-done.1, bf16[4,64,1024]{2,1,0:T(8,128)(2,1)S(1)} %copy-done, ...), custom_call_target="tpu_custom_call" | custom-call | flops 4000000000 | bytes 4000000 | tf_op jit(solution)/shard_map/pallas_call | solution.py:35
  25.7 1.6 %all-to-all-done.arrived = bf16[8,208,128]{2,1,0:T(8,128)(2,1)S(1)} async-done(((bf16[8,208,128]{2,1,0:T(8,128)(2,1)}), bf16[8,208,128]{2,1,0:T(8,128)(2,1)S(1)}, u32[]{:S(2)}, u32[]{:S(2)}) %all-to-all-start) | async-done | bytes 426016 | tf_op jit(solution)/shard_map/all_to_all | solution.py:367
  27.2 1.5 %shard_map.126 = (bf16[4,64,1024]{2,1,0:T(8,128)(2,1)}, f32[4,256]{1,0:T(4,128)}) custom-call(bf16[4,64,1024]{2,1,0:T(8,128)(2,1)S(1)} %copy-done.1, bf16[8,208,128]{2,1,0:T(8,128)(2,1)S(1)} %all-to-all-done.arrived, s32[4,256]{1,0:T(4,128)S(1)} %get-tuple-element.27.target, f32[4,64,512]{2,1,0:T(8,128)S(1)} %get-tuple-element.28.inner_base, ...), custom_call_target="tpu_custom_call" | custom-call | flops 3000000000 | bytes 3000000 | tf_op jit(solution)/shard_map/pallas_call | solution.py:35
  (1 shorter events, 0.0 us)
Async XLA Ops:
  0.6 1.6 %copy-start.3 = (bf16[4,128,256]{2,1,0:T(8,128)(2,1)S(1)}, bf16[4,128,256]{2,1,0:T(8,128)(2,1)}, u32[]{:S(2)}) copy-start(bf16[4,128,256]{2,1,0:T(8,128)(2,1)} %obs_lateral.1) | copy-start | bytes 786436
  0.6 1.6 %copy-start.5 = (bf16[4,64,256]{2,1,0:T(8,128)(2,1)S(1)}, bf16[4,64,256]{2,1,0:T(8,128)(2,1)}, u32[]{:S(2)}) copy-start(bf16[4,64,256]{2,1,0:T(8,128)(2,1)} %obs_vertical.1) | copy-start | bytes 393220
  0.7 1.6 %copy-start.8 = (bf16[4,256]{1,0:T(4,128)(2,1)S(1)}, bf16[4,256]{1,0:T(4,128)(2,1)}, u32[]{:S(2)}) copy-start(bf16[4,256]{1,0:T(4,128)(2,1)} %obs_weight.1) | copy-start | bytes 6148
  1.7 1.7 %copy-start = (bf16[4,64,1024]{2,1,0:T(8,128)(2,1)S(1)}, bf16[4,64,1024]{2,1,0:T(8,128)(2,1)}, u32[]{:S(2)}) copy-start(bf16[4,64,1024]{2,1,0:T(8,128)(2,1)} %costate.5) | copy-start | bytes 1572868
  1.7 1.7 %copy-start.1 = (bf16[4,64,1024]{2,1,0:T(8,128)(2,1)S(1)}, bf16[4,64,1024]{2,1,0:T(8,128)(2,1)}, u32[]{:S(2)}) copy-start(bf16[4,64,1024]{2,1,0:T(8,128)(2,1)} %incr.7) | copy-start | bytes 1572868
  1.7 1.7 %copy-start.7 = (s32[8,9]{1,0:T(8,128)S(1)}, s32[8,9]{1,0:T(8,128)}, u32[]{:S(2)}) copy-start(s32[8,9]{1,0:T(8,128)} %near.3) | copy-start | bytes 868
  1.7 1.6 %collective-permute-start = (bf16[64,1024]{1,0:T(8,128)(2,1)S(1)}, bf16[64,1024]{1,0:T(8,128)(2,1)S(1)}, u32[]{:S(2)}, u32[]{:S(2)}) collective-permute-start(bf16[64,1024]{1,0:T(8,128)(2,1)S(1)} %select_bitcast_fusion), channel_id=1, source_target_pairs={{0,1},{1,0},{2,3},{3,2},{4,5},{5,4},{6,7},{7,6},{8,9},{9,8},{10,11... | collective-permute-start | bytes 393224 | tf_op jit(solution)/shard_map/ppermute | solution.py:335
  3.7 16.4 %collective-permute-start.1 = (bf16[464,256]{1,0:T(8,128)(2,1)S(1)}, bf16[464,256]{1,0:T(8,128)(2,1)S(1)}, u32[]{:S(2)}, u32[]{:S(2)}) collective-permute-start(bf16[464,256]{1,0:T(8,128)(2,1)S(1)} %get-tuple-element.19.after), channel_id=1, source_target_pairs={{0,2},{4,6},{8,10},{12,14},{2,0},{6,4},{10,8},{14,12},{1,3},{5,7},... | collective-permute-start | bytes 712712 | tf_op jit(solution)/shard_map/ppermute | solution.py:30
  6.4 13.6 %collective-permute-start.2 = (bf16[464,256]{1,0:T(8,128)(2,1)S(1)}, bf16[464,256]{1,0:T(8,128)(2,1)S(1)}, u32[]{:S(2)}, u32[]{:S(2)}) collective-permute-start(bf16[464,256]{1,0:T(8,128)(2,1)S(1)} %get-tuple-element.20), channel_id=1, source_target_pairs={{2,4},{6,8},{10,12},{4,2},{8,6},{12,10},{3,5},{7,9},{11,13},{5,3},... | collective-permute-start | bytes 712712 | tf_op jit(solution)/shard_map/ppermute | solution.py:30
  7.1 7.8 %copy-start.2 = (bf16[9,128,128]{2,1,0:T(8,128)(2,1)S(1)}, bf16[9,128,128]{2,1,0:T(8,128)(2,1)}, u32[]{:S(2)}) copy-start(bf16[9,128,128]{2,1,0:T(8,128)(2,1)} %lateral_mix.1) | copy-start | bytes 884740
  7.1 7.8 %copy-start.4 = (bf16[9,64,64]{2,1,0:T(8,128)(2,1)S(1)}, bf16[9,64,64]{2,1,0:T(8,128)(2,1)}, u32[]{:S(2)}) copy-start(bf16[9,64,64]{2,1,0:T(8,128)(2,1)} %vertical_mix.1) | copy-start | bytes 221188
  7.2 7.8 %copy-start.6 = (s32[4,256]{1,0:T(4,128)S(1)}, s32[4,256]{1,0:T(4,128)}, u32[]{:S(2)}) copy-start(s32[4,256]{1,0:T(4,128)} %owner.1) | copy-start | bytes 12292
  7.2 7.8 %copy-start.9 = (s32[4,8]{1,0:T(4,128)S(1)}, s32[4,8]{1,0:T(4,128)}, u32[]{:S(2)}) copy-start(s32[4,8]{1,0:T(4,128)} %counts.1) | copy-start | bytes 388
  7.2 20.0 %all-to-all-start = ((bf16[8,208,128]{2,1,0:T(8,128)(2,1)}), bf16[8,208,128]{2,1,0:T(8,128)(2,1)S(1)}, u32[]{:S(2)}, u32[]{:S(2)}) async-start(bf16[8,208,128]{2,1,0:T(8,128)(2,1)} %shard_map.125), calls=%async_computation | async-start | bytes 851968 | tf_op jit(solution)/shard_map/all_to_all | solution.py:367

commit v6 on v5

--- a/solution.py
+++ b/solution.py
@@ -72,9 +72,9 @@
     fetch.wait()
     own = lax.broadcasted_iota(jnp.int32, near.shape, 0) + place * blocks
     distance = (near[...] - own).astype(F32)
-    distance = jnp.concatenate([distance, jnp.zeros((ROWS - blocks, entries), F32)], axis=0).astype(BF16)
+    distance = distance.astype(BF16)
     for target in (first, second):
-        target[len(slabs) * levels :] = jnp.zeros((ROWS, width), BF16)
+        target[len(slabs) * levels :] = jnp.zeros((blocks, width), BF16)
         target[len(slabs) * levels :, :entries] = distance
     for copy in copies:
         copy.wait()
@@ -223,7 +223,7 @@
         at = pl.ds(pl.multiple_of((near[b, j] - anchor + start) * cols, cols), cols)
         return before[s, :, at]
 
-    tail = slice((2 * moments - 1) * levels, (2 * moments - 1) * levels + ROWS)
+    tail = slice((2 * moments - 1) * levels, (2 * moments - 1) * levels + blocks)
     one, two = first[tail, :cols].astype(F32), second[tail, :cols].astype(F32)
     left = jnp.where(odd == 1, one, two)
     right = jnp.where(odd == 1, two, one)
@@ -352,7 +352,7 @@
         )
         outgoing = stacked.reshape(moments, height, tiles, cap).transpose(2, 1, 0, 3).reshape(tiles, height, -1)
 
-    halo = shape(((2 * moments - 1) * levels + ROWS, width), BF16)
+    halo = shape(((2 * moments - 1) * levels + blocks, width), BF16)
     first, second = call(
         edges_kernel,
         [halo, halo],

time: 29 us -> 29 us (level)
  no operation moved by 1% of the time
where the time goes in v6:
time: 29 us; the launch traced here: 28.7 us
  Pallas kernels  13.6 us (47%)
  starting transfers between devices  11.7 us (40%)
  waiting for transfers between devices  1.55 us (5%)
  other arithmetic  1.03 us (4%)
  between operations  0.84 us (3%)
    pallas_call x6, Pallas kernels, call(): pl.pallas_call(kernel, out_shape=out_shape, in_specs=specs, out_specs=out...  13.6 us
    all_to_all x1, starting transfers between devices, on_device(): lax.all_to_all(outgoing, 'space', split_axis=0, concat_axis=0, tiled=True)  7.72 us
    ppermute x2, starting transfers between devices, exchanged(): return lax.ppermute(array, 'space', both)  3.43 us
    all_to_all x1, waiting for transfers between devices, on_device(): lax.all_to_all(outgoing, 'space', split_axis=0, concat_axis=0, tiled=True)  1.54 us
    select_n x1, other arithmetic, on_device(): jnp.where(tm == 0, incr[-1], costate[0])  1.03 us
  transfers between devices with their start and end apart: 4, of which 1 were waited for; matrix products, arithmetic and copies ran while one was open for 0% of the time, Pallas kernels for 41%

profile of v6, /device:TPU:0, one launch (start us, length us, event | category | flops | bytes accessed | tf_op | source)
XLA Modules:
  0.0 28.7 jit_solution(2066683036399601530)
XLA Ops:
  0.6 0.0 copy-start.3
  0.6 0.0 copy-start.5
  0.7 0.0 copy-start.8
  0.7 1.0 %select_bitcast_fusion = bf16[64,1024]{1,0:T(8,128)(2,1)S(1)} fusion(bf16[4,64,1024]{2,1,0:T(8,128)(2,1)} %costate.5, bf16[4,64,1024]{2,1,0:T(8,128)(2,1)} %incr.7, pred[]{:T(512)S(6)} %eq.3), kind=kLoop, calls=%fused_computation | loop fusion | flops 65536 | bytes 393217 | tf_op jit(solution)/shard_map/jit(_where)/select_n | solution.py:335
  1.7 0.0 copy-start
  1.7 0.0 copy-start.1
  1.7 0.0 copy-start.7
  1.7 0.5 %collective-permute-start = (bf16[64,1024]{1,0:T(8,128)(2,1)S(1)}, bf16[64,1024]{1,0:T(8,128)(2,1)S(1)}, u32[]{:S(2)}, u32[]{:S(2)}) collective-permute-start(bf16[64,1024]{1,0:T(8,128)(2,1)S(1)} %select_bitcast_fusion), channel_id=1, source_target_pairs={{0,1},{1,0},{2,3},{3,2},{4,5},{5,4},{6,7},{7,6},{8,9},{9,8},{10,11... | collective-permute-start | bytes 393224 | tf_op jit(solution)/shard_map/ppermute | solution.py:335
  2.3 0.0 copy-done.3
  2.3 0.0 copy-done.5
  2.3 0.0 copy-done.8
  2.3 1.1 %shard_map.124.data = bf16[8,208,128]{2,1,0:T(8,128)(2,1)} custom-call(bf16[4,128,256]{2,1,0:T(8,128)(2,1)S(1)} %copy-done.3, bf16[4,64,256]{2,1,0:T(8,128)(2,1)S(1)} %copy-done.5, bf16[4,256]{1,0:T(4,128)(2,1)S(1)} %copy-done.8), custom_call_target="tpu_custom_call" | custom-call | flops 1000000000 | bytes 1000000 | tf_op jit(solution)/shard_map/pallas_call | solution.py:35
  3.4 0.0 collective-permute-done.crossed
  3.4 0.0 copy-done
  3.4 0.0 copy-done.1
  3.4 0.0 copy-done.7
  3.4 0.3 shard_map.121
  3.7 2.8 %collective-permute-start.1 = (bf16[456,256]{1,0:T(8,128)(2,1)S(1)}, bf16[456,256]{1,0:T(8,128)(2,1)S(1)}, u32[]{:S(2)}, u32[]{:S(2)}) collective-permute-start(bf16[456,256]{1,0:T(8,128)(2,1)S(1)} %get-tuple-element.19.after), channel_id=1, source_target_pairs={{0,2},{4,6},{8,10},{12,14},{2,0},{6,4},{10,8},{14,12},{1,3},{5,7},... | collective-permute-start | bytes 700424 | tf_op jit(solution)/shard_map/ppermute | solution.py:30
  6.4 0.7 %collective-permute-start.2 = (bf16[456,256]{1,0:T(8,128)(2,1)S(1)}, bf16[456,256]{1,0:T(8,128)(2,1)S(1)}, u32[]{:S(2)}, u32[]{:S(2)}) collective-permute-start(bf16[456,256]{1,0:T(8,128)(2,1)S(1)} %get-tuple-element.20), channel_id=1, source_target_pairs={{2,4},{6,8},{10,12},{4,2},{8,6},{12,10},{3,5},{7,9},{11,13},{5,3},... | collective-permute-start | bytes 700424 | tf_op jit(solution)/shard_map/ppermute | solution.py:30
  7.1 0.0 copy-start.2
  7.1 0.0 copy-start.4
  7.2 0.0 copy-start.6
  7.2 0.0 copy-start.9
  7.2 7.7 %all-to-all-start = ((bf16[8,208,128]{2,1,0:T(8,128)(2,1)}), bf16[8,208,128]{2,1,0:T(8,128)(2,1)S(1)}, u32[]{:S(2)}, u32[]{:S(2)}) async-start(bf16[8,208,128]{2,1,0:T(8,128)(2,1)} %shard_map.125), calls=%async_computation | async-start | bytes 851968 | tf_op jit(solution)/shard_map/all_to_all | solution.py:367
  14.9 0.0 copy-done.2
  14.9 0.0 copy-done.4
  14.9 0.0 copy-done.6
  14.9 0.0 copy-done.9
  14.9 5.1 %shard_map.122 = (bf16[4,64,512]{2,1,0:T(8,128)(2,1)S(1)}, f32[4,64,512]{2,1,0:T(8,128)S(1)}, bf16[5,256,256]{2,1,0:T(8,128)(2,1)S(1)}, bf16[5,256,256]{2,1,0:T(...) custom-call(s32[8,9]{1,0:T(8,128)S(1)} %copy-done.7, ...), custom_call_target="tpu_custom_call" | custom-call | flops 4000000000 | bytes 4000000 | tf_op jit(solution)/shard_map/pallas_call | solution.py:35
  20.1 0.0 collective-permute-done.1.first
  20.1 0.0 collective-permute-done.2.second
  20.1 5.6 %shard_map.123 = (bf16[4,64,1024]{2,1,0:T(8,128)(2,1)}, f32[64,512]{1,0:T(8,128)S(1)}, f32[64,512]{1,0:T(8,128)S(1)}, f32[64,512]{1,0:T(8,128)S(1)}, f32[64,512]{1,0:T(8,128)S(1)}) custom-call(s32[8,9]{1,0:T(8,128)S(1)} %copy-done.7, bf16[4,64,1024]{2,1,0:T(8,128)(2,1)S(1)} %copy-done.1, bf16[4,64,1024]{2,1,0:T(8,128)(2,1)S(1)} %copy-done, ...), custom_call_target="tpu_custom_call" | custom-call | flops 4000000000 | bytes 4000000 | tf_op jit(solution)/shard_map/pallas_call | solution.py:35
  25.7 1.5 %all-to-all-done.arrived = bf16[8,208,128]{2,1,0:T(8,128)(2,1)S(1)} async-done(((bf16[8,208,128]{2,1,0:T(8,128)(2,1)}), bf16[8,208,128]{2,1,0:T(8,128)(2,1)S(1)}, u32[]{:S(2)}, u32[]{:S(2)}) %all-to-all-start) | async-done | bytes 426016 | tf_op jit(solution)/shard_map/all_to_all | solution.py:367
  27.2 1.5 %shard_map.126 = (bf16[4,64,1024]{2,1,0:T(8,128)(2,1)}, f32[4,256]{1,0:T(4,128)}) custom-call(bf16[4,64,1024]{2,1,0:T(8,128)(2,1)S(1)} %copy-done.1, bf16[8,208,128]{2,1,0:T(8,128)(2,1)S(1)} %all-to-all-done.arrived, s32[4,256]{1,0:T(4,128)S(1)} %get-tuple-element.27.target, f32[4,64,512]{2,1,0:T(8,128)S(1)} %get-tuple-element.28.inner_base, ...), custom_call_target="tpu_custom_call" | custom-call | flops 3000000000 | bytes 3000000 | tf_op jit(solution)/shard_map/pallas_call | solution.py:35
  (1 shorter events, 0.0 us)
Async XLA Ops:
  0.6 1.6 %copy-start.3 = (bf16[4,128,256]{2,1,0:T(8,128)(2,1)S(1)}, bf16[4,128,256]{2,1,0:T(8,128)(2,1)}, u32[]{:S(2)}) copy-start(bf16[4,128,256]{2,1,0:T(8,128)(2,1)} %obs_lateral.1) | copy-start | bytes 786436
  0.6 1.6 %copy-start.5 = (bf16[4,64,256]{2,1,0:T(8,128)(2,1)S(1)}, bf16[4,64,256]{2,1,0:T(8,128)(2,1)}, u32[]{:S(2)}) copy-start(bf16[4,64,256]{2,1,0:T(8,128)(2,1)} %obs_vertical.1) | copy-start | bytes 393220
  0.7 1.6 %copy-start.8 = (bf16[4,256]{1,0:T(4,128)(2,1)S(1)}, bf16[4,256]{1,0:T(4,128)(2,1)}, u32[]{:S(2)}) copy-start(bf16[4,256]{1,0:T(4,128)(2,1)} %obs_weight.1) | copy-start | bytes 6148
  1.7 1.7 %copy-start = (bf16[4,64,1024]{2,1,0:T(8,128)(2,1)S(1)}, bf16[4,64,1024]{2,1,0:T(8,128)(2,1)}, u32[]{:S(2)}) copy-start(bf16[4,64,1024]{2,1,0:T(8,128)(2,1)} %costate.5) | copy-start | bytes 1572868
  1.7 1.7 %copy-start.1 = (bf16[4,64,1024]{2,1,0:T(8,128)(2,1)S(1)}, bf16[4,64,1024]{2,1,0:T(8,128)(2,1)}, u32[]{:S(2)}) copy-start(bf16[4,64,1024]{2,1,0:T(8,128)(2,1)} %incr.7) | copy-start | bytes 1572868
  1.7 1.7 %copy-start.7 = (s32[8,9]{1,0:T(8,128)S(1)}, s32[8,9]{1,0:T(8,128)}, u32[]{:S(2)}) copy-start(s32[8,9]{1,0:T(8,128)} %near.3) | copy-start | bytes 868
  1.7 1.6 %collective-permute-start = (bf16[64,1024]{1,0:T(8,128)(2,1)S(1)}, bf16[64,1024]{1,0:T(8,128)(2,1)S(1)}, u32[]{:S(2)}, u32[]{:S(2)}) collective-permute-start(bf16[64,1024]{1,0:T(8,128)(2,1)S(1)} %select_bitcast_fusion), channel_id=1, source_target_pairs={{0,1},{1,0},{2,3},{3,2},{4,5},{5,4},{6,7},{7,6},{8,9},{9,8},{10,11... | collective-permute-start | bytes 393224 | tf_op jit(solution)/shard_map/ppermute | solution.py:335
  3.7 16.4 %collective-permute-start.1 = (bf16[456,256]{1,0:T(8,128)(2,1)S(1)}, bf16[456,256]{1,0:T(8,128)(2,1)S(1)}, u32[]{:S(2)}, u32[]{:S(2)}) collective-permute-start(bf16[456,256]{1,0:T(8,128)(2,1)S(1)} %get-tuple-element.19.after), channel_id=1, source_target_pairs={{0,2},{4,6},{8,10},{12,14},{2,0},{6,4},{10,8},{14,12},{1,3},{5,7},... | collective-permute-start | bytes 700424 | tf_op jit(solution)/shard_map/ppermute | solution.py:30
  6.4 13.6 %collective-permute-start.2 = (bf16[456,256]{1,0:T(8,128)(2,1)S(1)}, bf16[456,256]{1,0:T(8,128)(2,1)S(1)}, u32[]{:S(2)}, u32[]{:S(2)}) collective-permute-start(bf16[456,256]{1,0:T(8,128)(2,1)S(1)} %get-tuple-element.20), channel_id=1, source_target_pairs={{2,4},{6,8},{10,12},{4,2},{8,6},{12,10},{3,5},{7,9},{11,13},{5,3},... | collective-permute-start | bytes 700424 | tf_op jit(solution)/shard_map/ppermute | solution.py:30
  7.1 7.8 %copy-start.2 = (bf16[9,128,128]{2,1,0:T(8,128)(2,1)S(1)}, bf16[9,128,128]{2,1,0:T(8,128)(2,1)}, u32[]{:S(2)}) copy-start(bf16[9,128,128]{2,1,0:T(8,128)(2,1)} %lateral_mix.1) | copy-start | bytes 884740
  7.1 7.8 %copy-start.4 = (bf16[9,64,64]{2,1,0:T(8,128)(2,1)S(1)}, bf16[9,64,64]{2,1,0:T(8,128)(2,1)}, u32[]{:S(2)}) copy-start(bf16[9,64,64]{2,1,0:T(8,128)(2,1)} %vertical_mix.1) | copy-start | bytes 221188
  7.2 7.8 %copy-start.6 = (s32[4,256]{1,0:T(4,128)S(1)}, s32[4,256]{1,0:T(4,128)}, u32[]{:S(2)}) copy-start(s32[4,256]{1,0:T(4,128)} %owner.1) | copy-start | bytes 12292
  7.2 7.8 %copy-start.9 = (s32[4,8]{1,0:T(4,128)S(1)}, s32[4,8]{1,0:T(4,128)}, u32[]{:S(2)}) copy-start(s32[4,8]{1,0:T(4,128)} %counts.1) | copy-start | bytes 388
  7.2 20.0 %all-to-all-start = ((bf16[8,208,128]{2,1,0:T(8,128)(2,1)}), bf16[8,208,128]{2,1,0:T(8,128)(2,1)S(1)}, u32[]{:S(2)}, u32[]{:S(2)}) async-start(bf16[8,208,128]{2,1,0:T(8,128)(2,1)} %shard_map.125), calls=%async_computation | async-start | bytes 851968 | tf_op jit(solution)/shard_map/all_to_all | solution.py:367

commit v7 on v5

--- a/solution.py
+++ b/solution.py
@@ -299,12 +299,6 @@
         vertical = whole[cols : cols + levels].astype(F32)
         weight = whole[cols + levels :].astype(F32)[:1]
         hits = [jnp.where(block == b, 1.0, 0.0) for b in range(blocks)]
-        fields = jnp.concatenate([incr[s, :, b * cols : (b + 1) * cols] for b in range(blocks)], axis=0)
-        seen = dot(fields, lateral)
-        along = sum(hits[b] * seen[b * levels : (b + 1) * levels] for b in range(blocks))
-        image[s : s + 1] = jnp.sum(vertical * along, axis=0, keepdims=True)
-        if s == moments - 1:
-            copies += fetched([(image, image_any)], sems.at[pl.ds(moments, 1)])
         scaled = (vertical * weight).astype(BF16)
         parts = [scaled * jnp.broadcast_to(hit, scaled.shape).astype(BF16) for hit in hits]
         stacked = dot_nt(jnp.concatenate(parts, axis=0), lateral)
@@ -313,6 +307,12 @@
         adjoint[s, :, inner_lanes] = (inner_base[s] + push[:, inner_lanes]).astype(BF16)
         adjoint[s, :, cols_all - width :] = (outer_base[s][:, width:] + push[:, cols_all - width :]).astype(BF16)
         copies += fetched([(adjoint.at[s], adjoint_any.at[s])], sems.at[pl.ds(s, 1)])
+        fields = jnp.concatenate([incr[s, :, b * cols : (b + 1) * cols] for b in range(blocks)], axis=0)
+        seen = dot(fields, lateral)
+        along = sum(hits[b] * seen[b * levels : (b + 1) * levels] for b in range(blocks))
+        image[s : s + 1] = jnp.sum(vertical * along, axis=0, keepdims=True)
+        if s == moments - 1:
+            copies += fetched([(image, image_any)], sems.at[pl.ds(moments, 1)])
     for copy in copies:
         copy.wait()
 

time: 29 us -> 29 us (level)
  no operation moved by 1% of the time
where the time goes in v7:
time: 29 us; the launch traced here: 28.7 us
  Pallas kernels  13.6 us (47%)
  starting transfers between devices  11.7 us (40%)
  waiting for transfers between devices  1.56 us (5%)
  other arithmetic  1.03 us (4%)
  between operations  0.84 us (3%)
    pallas_call x6, Pallas kernels, call(): pl.pallas_call(kernel, out_shape=out_shape, in_specs=specs, out_specs=out...  13.6 us
    all_to_all x1, starting transfers between devices, on_device(): lax.all_to_all(outgoing, 'space', split_axis=0, concat_axis=0, tiled=True)  7.72 us
    ppermute x2, starting transfers between devices, exchanged(): return lax.ppermute(array, 'space', both)  3.43 us
    all_to_all x1, waiting for transfers between devices, on_device(): lax.all_to_all(outgoing, 'space', split_axis=0, concat_axis=0, tiled=True)  1.55 us
    select_n x1, other arithmetic, on_device(): jnp.where(tm == 0, incr[-1], costate[0])  1.03 us
  transfers between devices with their start and end apart: 4, of which 1 were waited for; matrix products, arithmetic and copies ran while one was open for 0% of the time, Pallas kernels for 41%

profile of v7, /device:TPU:0, one launch (start us, length us, event | category | flops | bytes accessed | tf_op | source)
XLA Modules:
  0.0 28.7 jit_solution(1531140563069333499)
XLA Ops:
  0.6 0.0 copy-start.3
  0.6 0.0 copy-start.5
  0.7 0.0 copy-start.8
  0.7 1.0 %select_bitcast_fusion = bf16[64,1024]{1,0:T(8,128)(2,1)S(1)} fusion(bf16[4,64,1024]{2,1,0:T(8,128)(2,1)} %costate.5, bf16[4,64,1024]{2,1,0:T(8,128)(2,1)} %incr.7, pred[]{:T(512)S(6)} %eq.3), kind=kLoop, calls=%fused_computation | loop fusion | flops 65536 | bytes 393217 | tf_op jit(solution)/shard_map/jit(_where)/select_n | solution.py:335
  1.7 0.0 copy-start
  1.7 0.0 copy-start.1
  1.7 0.0 copy-start.7
  1.7 0.5 %collective-permute-start = (bf16[64,1024]{1,0:T(8,128)(2,1)S(1)}, bf16[64,1024]{1,0:T(8,128)(2,1)S(1)}, u32[]{:S(2)}, u32[]{:S(2)}) collective-permute-start(bf16[64,1024]{1,0:T(8,128)(2,1)S(1)} %select_bitcast_fusion), channel_id=1, source_target_pairs={{0,1},{1,0},{2,3},{3,2},{4,5},{5,4},{6,7},{7,6},{8,9},{9,8},{10,11... | collective-permute-start | bytes 393224 | tf_op jit(solution)/shard_map/ppermute | solution.py:335
  2.3 0.0 copy-done.3
  2.3 0.0 copy-done.5
  2.3 0.0 copy-done.8
  2.3 1.1 %shard_map.124.data = bf16[8,208,128]{2,1,0:T(8,128)(2,1)} custom-call(bf16[4,128,256]{2,1,0:T(8,128)(2,1)S(1)} %copy-done.3, bf16[4,64,256]{2,1,0:T(8,128)(2,1)S(1)} %copy-done.5, bf16[4,256]{1,0:T(4,128)(2,1)S(1)} %copy-done.8), custom_call_target="tpu_custom_call" | custom-call | flops 1000000000 | bytes 1000000 | tf_op jit(solution)/shard_map/pallas_call | solution.py:35
  3.4 0.0 collective-permute-done.crossed
  3.4 0.0 copy-done
  3.4 0.0 copy-done.1
  3.4 0.0 copy-done.7
  3.4 0.3 shard_map.121
  3.7 2.8 %collective-permute-start.1 = (bf16[464,256]{1,0:T(8,128)(2,1)S(1)}, bf16[464,256]{1,0:T(8,128)(2,1)S(1)}, u32[]{:S(2)}, u32[]{:S(2)}) collective-permute-start(bf16[464,256]{1,0:T(8,128)(2,1)S(1)} %get-tuple-element.19.after), channel_id=1, source_target_pairs={{0,2},{4,6},{8,10},{12,14},{2,0},{6,4},{10,8},{14,12},{1,3},{5,7},... | collective-permute-start | bytes 712712 | tf_op jit(solution)/shard_map/ppermute | solution.py:30
  6.4 0.7 %collective-permute-start.2 = (bf16[464,256]{1,0:T(8,128)(2,1)S(1)}, bf16[464,256]{1,0:T(8,128)(2,1)S(1)}, u32[]{:S(2)}, u32[]{:S(2)}) collective-permute-start(bf16[464,256]{1,0:T(8,128)(2,1)S(1)} %get-tuple-element.20), channel_id=1, source_target_pairs={{2,4},{6,8},{10,12},{4,2},{8,6},{12,10},{3,5},{7,9},{11,13},{5,3},... | collective-permute-start | bytes 712712 | tf_op jit(solution)/shard_map/ppermute | solution.py:30
  7.1 0.0 copy-start.2
  7.1 0.0 copy-start.4
  7.2 0.0 copy-start.6
  7.2 0.0 copy-start.9
  7.2 7.7 %all-to-all-start = ((bf16[8,208,128]{2,1,0:T(8,128)(2,1)}), bf16[8,208,128]{2,1,0:T(8,128)(2,1)S(1)}, u32[]{:S(2)}, u32[]{:S(2)}) async-start(bf16[8,208,128]{2,1,0:T(8,128)(2,1)} %shard_map.125), calls=%async_computation | async-start | bytes 851968 | tf_op jit(solution)/shard_map/all_to_all | solution.py:367
  14.9 0.0 copy-done.2
  14.9 0.0 copy-done.4
  14.9 0.0 copy-done.6
  14.9 0.0 copy-done.9
  14.9 5.1 %shard_map.122 = (bf16[4,64,512]{2,1,0:T(8,128)(2,1)S(1)}, f32[4,64,512]{2,1,0:T(8,128)S(1)}, bf16[5,256,256]{2,1,0:T(8,128)(2,1)S(1)}, bf16[5,256,256]{2,1,0:T(...) custom-call(s32[8,9]{1,0:T(8,128)S(1)} %copy-done.7, ...), custom_call_target="tpu_custom_call" | custom-call | flops 4000000000 | bytes 4000000 | tf_op jit(solution)/shard_map/pallas_call | solution.py:35
  20.0 0.0 collective-permute-done.1.first
  20.1 0.0 collective-permute-done.2.second
  20.1 5.6 %shard_map.123 = (bf16[4,64,1024]{2,1,0:T(8,128)(2,1)}, f32[64,512]{1,0:T(8,128)S(1)}, f32[64,512]{1,0:T(8,128)S(1)}, f32[64,512]{1,0:T(8,128)S(1)}, f32[64,512]{1,0:T(8,128)S(1)}) custom-call(s32[8,9]{1,0:T(8,128)S(1)} %copy-done.7, bf16[4,64,1024]{2,1,0:T(8,128)(2,1)S(1)} %copy-done.1, bf16[4,64,1024]{2,1,0:T(8,128)(2,1)S(1)} %copy-done, ...), custom_call_target="tpu_custom_call" | custom-call | flops 4000000000 | bytes 4000000 | tf_op jit(solution)/shard_map/pallas_call | solution.py:35
  25.7 1.6 %all-to-all-done.arrived = bf16[8,208,128]{2,1,0:T(8,128)(2,1)S(1)} async-done(((bf16[8,208,128]{2,1,0:T(8,128)(2,1)}), bf16[8,208,128]{2,1,0:T(8,128)(2,1)S(1)}, u32[]{:S(2)}, u32[]{:S(2)}) %all-to-all-start) | async-done | bytes 426016 | tf_op jit(solution)/shard_map/all_to_all | solution.py:367
  27.2 1.5 %shard_map.126 = (bf16[4,64,1024]{2,1,0:T(8,128)(2,1)}, f32[4,256]{1,0:T(4,128)}) custom-call(bf16[4,64,1024]{2,1,0:T(8,128)(2,1)S(1)} %copy-done.1, bf16[8,208,128]{2,1,0:T(8,128)(2,1)S(1)} %all-to-all-done.arrived, s32[4,256]{1,0:T(4,128)S(1)} %get-tuple-element.27.target, f32[4,64,512]{2,1,0:T(8,128)S(1)} %get-tuple-element.28.inner_base, ...), custom_call_target="tpu_custom_call" | custom-call | flops 3000000000 | bytes 3000000 | tf_op jit(solution)/shard_map/pallas_call | solution.py:35
  (1 shorter events, 0.0 us)
Async XLA Ops:
  0.6 1.6 %copy-start.3 = (bf16[4,128,256]{2,1,0:T(8,128)(2,1)S(1)}, bf16[4,128,256]{2,1,0:T(8,128)(2,1)}, u32[]{:S(2)}) copy-start(bf16[4,128,256]{2,1,0:T(8,128)(2,1)} %obs_lateral.1) | copy-start | bytes 786436
  0.6 1.6 %copy-start.5 = (bf16[4,64,256]{2,1,0:T(8,128)(2,1)S(1)}, bf16[4,64,256]{2,1,0:T(8,128)(2,1)}, u32[]{:S(2)}) copy-start(bf16[4,64,256]{2,1,0:T(8,128)(2,1)} %obs_vertical.1) | copy-start | bytes 393220
  0.7 1.6 %copy-start.8 = (bf16[4,256]{1,0:T(4,128)(2,1)S(1)}, bf16[4,256]{1,0:T(4,128)(2,1)}, u32[]{:S(2)}) copy-start(bf16[4,256]{1,0:T(4,128)(2,1)} %obs_weight.1) | copy-start | bytes 6148
  1.7 1.7 %copy-start = (bf16[4,64,1024]{2,1,0:T(8,128)(2,1)S(1)}, bf16[4,64,1024]{2,1,0:T(8,128)(2,1)}, u32[]{:S(2)}) copy-start(bf16[4,64,1024]{2,1,0:T(8,128)(2,1)} %costate.5) | copy-start | bytes 1572868
  1.7 1.7 %copy-start.1 = (bf16[4,64,1024]{2,1,0:T(8,128)(2,1)S(1)}, bf16[4,64,1024]{2,1,0:T(8,128)(2,1)}, u32[]{:S(2)}) copy-start(bf16[4,64,1024]{2,1,0:T(8,128)(2,1)} %incr.7) | copy-start | bytes 1572868
  1.7 1.7 %copy-start.7 = (s32[8,9]{1,0:T(8,128)S(1)}, s32[8,9]{1,0:T(8,128)}, u32[]{:S(2)}) copy-start(s32[8,9]{1,0:T(8,128)} %near.3) | copy-start | bytes 868
  1.7 1.6 %collective-permute-start = (bf16[64,1024]{1,0:T(8,128)(2,1)S(1)}, bf16[64,1024]{1,0:T(8,128)(2,1)S(1)}, u32[]{:S(2)}, u32[]{:S(2)}) collective-permute-start(bf16[64,1024]{1,0:T(8,128)(2,1)S(1)} %select_bitcast_fusion), channel_id=1, source_target_pairs={{0,1},{1,0},{2,3},{3,2},{4,5},{5,4},{6,7},{7,6},{8,9},{9,8},{10,11... | collective-permute-start | bytes 393224 | tf_op jit(solution)/shard_map/ppermute | solution.py:335
  3.7 16.4 %collective-permute-start.1 = (bf16[464,256]{1,0:T(8,128)(2,1)S(1)}, bf16[464,256]{1,0:T(8,128)(2,1)S(1)}, u32[]{:S(2)}, u32[]{:S(2)}) collective-permute-start(bf16[464,256]{1,0:T(8,128)(2,1)S(1)} %get-tuple-element.19.after), channel_id=1, source_target_pairs={{0,2},{4,6},{8,10},{12,14},{2,0},{6,4},{10,8},{14,12},{1,3},{5,7},... | collective-permute-start | bytes 712712 | tf_op jit(solution)/shard_map/ppermute | solution.py:30
  6.4 13.6 %collective-permute-start.2 = (bf16[464,256]{1,0:T(8,128)(2,1)S(1)}, bf16[464,256]{1,0:T(8,128)(2,1)S(1)}, u32[]{:S(2)}, u32[]{:S(2)}) collective-permute-start(bf16[464,256]{1,0:T(8,128)(2,1)S(1)} %get-tuple-element.20), channel_id=1, source_target_pairs={{2,4},{6,8},{10,12},{4,2},{8,6},{12,10},{3,5},{7,9},{11,13},{5,3},... | collective-permute-start | bytes 712712 | tf_op jit(solution)/shard_map/ppermute | solution.py:30
  7.1 7.8 %copy-start.2 = (bf16[9,128,128]{2,1,0:T(8,128)(2,1)S(1)}, bf16[9,128,128]{2,1,0:T(8,128)(2,1)}, u32[]{:S(2)}) copy-start(bf16[9,128,128]{2,1,0:T(8,128)(2,1)} %lateral_mix.1) | copy-start | bytes 884740
  7.1 7.8 %copy-start.4 = (bf16[9,64,64]{2,1,0:T(8,128)(2,1)S(1)}, bf16[9,64,64]{2,1,0:T(8,128)(2,1)}, u32[]{:S(2)}) copy-start(bf16[9,64,64]{2,1,0:T(8,128)(2,1)} %vertical_mix.1) | copy-start | bytes 221188
  7.2 7.8 %copy-start.6 = (s32[4,256]{1,0:T(4,128)S(1)}, s32[4,256]{1,0:T(4,128)}, u32[]{:S(2)}) copy-start(s32[4,256]{1,0:T(4,128)} %owner.1) | copy-start | bytes 12292
  7.2 7.8 %copy-start.9 = (s32[4,8]{1,0:T(4,128)S(1)}, s32[4,8]{1,0:T(4,128)}, u32[]{:S(2)}) copy-start(s32[4,8]{1,0:T(4,128)} %counts.1) | copy-start | bytes 388
  7.2 20.0 %all-to-all-start = ((bf16[8,208,128]{2,1,0:T(8,128)(2,1)}), bf16[8,208,128]{2,1,0:T(8,128)(2,1)S(1)}, u32[]{:S(2)}, u32[]{:S(2)}) async-start(bf16[8,208,128]{2,1,0:T(8,128)(2,1)} %shard_map.125), calls=%async_computation | async-start | bytes 851968 | tf_op jit(solution)/shard_map/all_to_all | solution.py:367
